TPU v7x, 32 devices: a whole 2x2x4 slice. The times are simulated.
32 devices in a mesh: dp: 8 (over z, x), tensor: 4 (over y, core).
Axes of the slice: x: 2, y: 2, z: 4, core: 2. Of those that a mesh axis runs over, the one named last changes fastest.
Arguments:
- block_input: bfloat16 [16384, 768], P(('dp', 'tensor')), may hold values from -6 to 6
- out_grad: bfloat16 [16384, 768], P(('dp', 'tensor')), may hold values from -6 to 6
- w_qkv: bfloat16 [3, 768, 768], P(None, 'dp', 'tensor'), may hold values from -0.21875 to 0.21875
- w_out: bfloat16 [768, 768], P('tensor', 'dp'), may hold values from -0.875 to 0.875
- rel_table: float32 [32, 12], replicated, may hold values from -4 to 4
- gain_attn: float32 [768], replicated, may hold values from 0.5 to 1.5
- gain_moe: float32 [768], replicated, may hold values from 0.5 to 1.5
- w_router: bfloat16 [768, 8], replicated, may hold values from -0.15917969 to 0.15917969
- w_up: bfloat16 [8, 3072, 768], P('dp', 'tensor'), may hold values from -0.21875 to 0.21875
- w_down: bfloat16 [8, 3072, 768], P('dp', 'tensor'), may hold values from -0.21875 to 0.21875
- routes: int32 [16384, 2], P(('dp', 'tensor')), may hold values from 0 to 7, all different within a row
- segments: int32 [16, 1024], P('dp'), may hold values from 0 to 510, as said below
- padding: int32 [16, 1024], P('dp'), may hold values from 0 to 1, as said below
- rel_bucket: int32 [1024], replicated, may hold values from 0 to 31, as said below
Outputs:
- block_output: float32 [16384, 768], P(('dp', 'tensor'))
- input_grad: float32 [16384, 768], P(('dp', 'tensor'))
- w_qkv_grad: float32 [3, 768, 768], P(None, 'dp', 'tensor')
- w_out_grad: float32 [768, 768], P('tensor', 'dp')
- rel_table_grad: float32 [32, 12], replicated
- gain_attn_grad: float32 [768], replicated
- gain_moe_grad: float32 [768], replicated
- w_router_grad: float32 [768, 8], replicated
- w_up_grad: float32 [8, 3072, 768], P('dp', 'tensor')
- w_down_grad: float32 [8, 3072, 768], P('dp', 'tensor')
Inputs may be any that keep to these rules, and one draw needn't show every extreme that they name: `segments`: along a sequence the ids never fall; places 1024 // 4 to 768 belong to one document; the first document has id 0 and the last one, which holds at least place 1024 - 1, has id 1024 // 2 - 2. `padding`: each sequence is ones followed by at most 128 zeros. `rel_bucket`: distance 0 has bucket 0, buckets never fall with distance, distance 1024 - 1 has bucket 32 - 1. `routes`: A token's two experts differ.
All inputs are finite; a program needn't handle non-finite values.
Results may differ from a plain program's by a relative error of at most 0.015.
Values may be sent and summed in bfloat16 or wider, within the bound.
A program may use at most 256 MiB of HBM per device.

v0:
```python
import functools
import math

import jax
import jax.numpy as jnp
from jax import lax
from jax.experimental import pallas as pl
from jax.experimental.pallas import tpu as pltpu
from jax.sharding import PartitionSpec as P

NB = 32
EPSILON = 1e-06
HIGHEST = lax.Precision.HIGHEST
DH = 64
NEGATIVE = -1e30
QB = 256
NT = (((1,), (1,)), ((), ()))
TN = (((0,), (0,)), ((), ()))
NN = (((1,), (0,)), ((), ()))


def mm(a, b, dims):
    return lax.dot_general(a, b, dims, preferred_element_type=jnp.float32)


def build_bias(line_ref, tiles, heads, blocks):
    for h in range(heads):
        for d in range(blocks):
            piece = line_ref[h : h + 1, d * QB : d * QB + 2 * QB]
            wide = jnp.broadcast_to(piece, (QB, 2 * QB))
            turned = pltpu.roll(wide, 0, 1, stride=1, stride_axis=0)
            tiles[h, d] = turned[:, QB:]


def score_block(keys, query, tiles, h, qb, segk_ref, segq_ref):
    raw = mm(keys, query, NT)
    q_seg = segq_ref[0, :, qb * QB : (qb + 1) * QB]
    parts = []
    for kb in range(qb + 1):
        k_seg = segk_ref[0, kb * QB : (kb + 1) * QB, :]
        same = k_seg == q_seg
        if kb == qb:
            row = lax.broadcasted_iota(jnp.int32, (QB, QB), 0)
            col = lax.broadcasted_iota(jnp.int32, (QB, QB), 1)
            same = same | (row == col)
        parts.append(
            jnp.where(same, raw[kb * QB : (kb + 1) * QB] + tiles[h, qb - kb], NEGATIVE)
        )
    return parts


def attend_kernel(heads, blocks, line_ref, segk_ref, segq_ref, rows_ref, w_ref,
                  qkv_ref, out_ref, lse_ref, tiles):
    @pl.when(pl.program_id(0) == 0)
    def _():
        build_bias(line_ref, tiles, heads, blocks)

    for c in range(3):
        qkv_ref[c] = mm(rows_ref[...], w_ref[c], NN).astype(jnp.bfloat16)
    scale = 1.0 / math.sqrt(DH)
    for qb in range(blocks):
        nk = (qb + 1) * QB
        lower = qb * QB
        turned = []
        for h in range(heads):
            cols = slice(h * DH, (h + 1) * DH)
            query = (qkv_ref[0, lower : lower + QB, cols].astype(jnp.float32) * scale).astype(jnp.bfloat16)
            parts = score_block(qkv_ref[1, 0:nk, cols], query, tiles, h, qb, segk_ref, segq_ref)
            peak = functools.reduce(jnp.maximum, [jnp.max(x, axis=0, keepdims=True) for x in parts])
            probs = [jnp.exp(x - peak) for x in parts]
            total = functools.reduce(jnp.add, [jnp.sum(x, axis=0, keepdims=True) for x in probs])
            mixed = functools.reduce(jnp.add, [
                mm(qkv_ref[2, kb * QB : (kb + 1) * QB, cols], x.astype(jnp.bfloat16), TN)
                for kb, x in enumerate(probs)])
            turned.append(mixed / total)
            lse_ref[0, h : h + 1, lower : lower + QB] = peak + jnp.log(total)
        out_ref[lower : lower + QB, :] = jnp.concatenate(turned, axis=0).T.astype(jnp.bfloat16)


def attend(line, segk, segq, rows, w):
    seqs, _, seq_len = segq.shape
    heads = line.shape[0]
    inner = heads * DH
    blocks = seq_len // QB
    width = rows.shape[1]
    return pl.pallas_call(
        functools.partial(attend_kernel, heads, blocks),
        grid=(seqs,),
        in_specs=[
            pl.BlockSpec(line.shape, lambda s: (0, 0)),
            pl.BlockSpec((1, seq_len, 1), lambda s: (s, 0, 0)),
            pl.BlockSpec((1, 1, seq_len), lambda s: (s, 0, 0)),
            pl.BlockSpec((seq_len, width), lambda s: (s, 0)),
            pl.BlockSpec(w.shape, lambda s: (0, 0, 0)),
        ],
        out_specs=[
            pl.BlockSpec((3, seq_len, inner), lambda s: (0, s, 0)),
            pl.BlockSpec((seq_len, inner), lambda s: (s, 0)),
            pl.BlockSpec((1, heads, seq_len), lambda s: (s, 0, 0)),
        ],
        out_shape=[
            jax.ShapeDtypeStruct((3, seqs * seq_len, inner), jnp.bfloat16),
            jax.ShapeDtypeStruct((seqs * seq_len, inner), jnp.bfloat16),
            jax.ShapeDtypeStruct((seqs, heads, seq_len), jnp.float32),
        ],
        scratch_shapes=[pltpu.VMEM((heads, blocks, QB, QB), jnp.float32)],
        compiler_params=pltpu.CompilerParams(vmem_limit_bytes=48 << 20),
        cost_estimate=pl.CostEstimate(flops=10_000_000_000, bytes_accessed=10 << 20, transcendentals=4_000_000),
        name="attend",
    )(line, segk, segq, rows, w)


def attend_back_kernel(heads, blocks, seqs, line_ref, segk_ref, segq_ref, rows_ref, w_ref,
                       qkv_ref, og_ref, lse_ref,
                       norm_ref, wg_ref, lg_ref, tiles, sums, kg, vg, dq):
    step = pl.program_id(0)

    @pl.when(step == 0)
    def _():
        build_bias(line_ref, tiles, heads, blocks)
        sums[...] = jnp.zeros_like(sums)
        wg_ref[...] = jnp.zeros_like(wg_ref)

    scale = 1.0 / math.sqrt(DH)
    for h in range(heads):
        cols = slice(h * DH, (h + 1) * DH)
        kg[...] = jnp.zeros_like(kg)
        vg[...] = jnp.zeros_like(vg)
        for qb in range(blocks):
            nk = (qb + 1) * QB
            lower = qb * QB
            query = (qkv_ref[0, lower : lower + QB, cols].astype(jnp.float32) * scale).astype(jnp.bfloat16)
            grad = og_ref[lower : lower + QB, cols]
            lse = lse_ref[0, h : h + 1, lower : lower + QB]
            parts = score_block(qkv_ref[1, 0:nk, cols], query, tiles, h, qb, segk_ref, segq_ref)
            probs = [jnp.exp(x - lse) for x in parts]
            pg = mm(qkv_ref[2, 0:nk, cols], grad, NT)
            pgs = [pg[kb * QB : (kb + 1) * QB] for kb in range(qb + 1)]
            delta = functools.reduce(jnp.add, [jnp.sum(p * g, axis=0, keepdims=True) for p, g in zip(probs, pgs)])
            dqt = jnp.zeros((DH, QB), jnp.float32)
            for kb in range(qb + 1):
                rows = slice(kb * QB, (kb + 1) * QB)
                sg = (probs[kb] * (pgs[kb] - delta)).astype(jnp.bfloat16)
                sums[h, qb - kb] += sg.astype(jnp.float32)
                vg[rows] += mm(probs[kb].astype(jnp.bfloat16), grad, NN)
                kg[rows] += mm(sg, query, NN)
                dqt = dqt + mm(qkv_ref[1, rows, cols], sg, TN)
            dq[lower : lower + QB, h * DH : (h + 1) * DH] = (dqt * scale).T.astype(jnp.bfloat16)
        inner = heads * DH
        dq[:, inner + h * DH : inner + (h + 1) * DH] = kg[...].astype(jnp.bfloat16)
        dq[:, 2 * inner + h * DH : 2 * inner + (h + 1) * DH] = vg[...].astype(jnp.bfloat16)
    inner = heads * DH
    total = jnp.zeros(norm_ref.shape, jnp.float32)
    for c in range(3):
        piece = dq[:, c * inner : (c + 1) * inner]
        wg_ref[c] += mm(rows_ref[...], piece, TN)
        total = total + mm(piece, w_ref[c], NT)
    norm_ref[...] = total.astype(norm_ref.dtype)

    @pl.when(step == seqs - 1)
    def _():
        for h in range(heads):
            for d in range(blocks):
                lg_ref[h * blocks + d] = fold_tile(sums, h, d)


def fold_tile(sums, h, d):
    blank = jnp.zeros((8, QB), jnp.float32)
    total = jnp.zeros((8, 2 * QB), jnp.float32)
    for g in range(QB // 8):
        piece = jnp.concatenate([sums[h, d, 8 * g : 8 * g + 8, :], blank], axis=1)
        total = total + (piece if g == 0 else pltpu.roll(piece, 2 * QB - 8 * g, 1))
    return total


def lines_of(folded, heads, blocks):
    moved = sum(jnp.roll(folded[:, s, :], -s, axis=1) for s in range(8))
    moved = moved.reshape(heads, blocks, 2, QB)
    ahead = jnp.concatenate([moved[:, 1:, 1], jnp.zeros((heads, 1, QB), jnp.float32)], axis=1)
    return (moved[:, :, 0] + ahead).reshape(heads, blocks * QB)


def attend_back(line, segk, segq, rows, w, qkv, og, lse):
    seqs, _, seq_len = segq.shape
    heads = line.shape[0]
    inner = heads * DH
    blocks = seq_len // QB
    width = rows.shape[1]
    return pl.pallas_call(
        functools.partial(attend_back_kernel, heads, blocks, seqs),
        grid=(seqs,),
        in_specs=[
            pl.BlockSpec(line.shape, lambda s: (0, 0)),
            pl.BlockSpec((1, seq_len, 1), lambda s: (s, 0, 0)),
            pl.BlockSpec((1, 1, seq_len), lambda s: (s, 0, 0)),
            pl.BlockSpec((seq_len, width), lambda s: (s, 0)),
            pl.BlockSpec(w.shape, lambda s: (0, 0, 0)),
            pl.BlockSpec((3, seq_len, inner), lambda s: (0, s, 0)),
            pl.BlockSpec((seq_len, inner), lambda s: (s, 0)),
            pl.BlockSpec((1, heads, seq_len), lambda s: (s, 0, 0)),
        ],
        out_specs=[
            pl.BlockSpec((seq_len, width), lambda s: (s, 0)),
            pl.BlockSpec(w.shape, lambda s: (0, 0, 0)),
            pl.BlockSpec((heads * blocks, 8, 2 * QB), lambda s: (0, 0, 0)),
        ],
        out_shape=[
            jax.ShapeDtypeStruct((seqs * seq_len, width), jnp.bfloat16),
            jax.ShapeDtypeStruct(w.shape, jnp.float32),
            jax.ShapeDtypeStruct((heads * blocks, 8, 2 * QB), jnp.float32),
        ],
        scratch_shapes=[
            pltpu.VMEM((heads, blocks, QB, QB), jnp.float32),
            pltpu.VMEM((heads, blocks, QB, QB), jnp.float32),
            pltpu.VMEM((seq_len, DH), jnp.float32),
            pltpu.VMEM((seq_len, DH), jnp.float32),
            pltpu.VMEM((seq_len, 3 * inner), jnp.bfloat16),
        ],
        compiler_params=pltpu.CompilerParams(vmem_limit_bytes=48 << 20),
        cost_estimate=pl.CostEstimate(flops=20_000_000_000, bytes_accessed=16 << 20, transcendentals=4_000_000),
        name="attend_back",
    )(line, segk, segq, rows, w, qkv, og, lse)


def mask_inputs(segments, padding):
    keyed = jnp.where(padding == 1, segments, -1)
    return keyed[:, :, None], segments[:, None, :]


def line_of(by_distance):
    return jnp.concatenate([jnp.full((by_distance.shape[0], QB), NEGATIVE, jnp.float32), by_distance], axis=1)


FT = 512
ROOT_2_PI = math.sqrt(2.0 / math.pi)


def gelu_pair(x):
    square = x * x
    t = jnp.tanh(ROOT_2_PI * x * (1.0 + 0.044715 * square))
    half = 0.5 * (1.0 + t)
    slope = half + 0.5 * x * (1.0 - t * t) * (ROOT_2_PI * (1.0 + 3 * 0.044715 * square))
    return x * half, slope


def expert_kernel(steps, x_ref, g_ref, up_ref, down_ref, act_ref, pre_ref, back_ref, dot_ref, total, dots):
    step = pl.program_id(0)

    @pl.when(step == 0)
    def _():
        total[...] = jnp.zeros_like(total)
        dots[...] = jnp.zeros_like(dots)

    rows = x_ref.shape[0]
    chunk = 256
    for lower in range(0, rows, chunk):
        part = slice(lower, lower + chunk)
        pre = mm(x_ref[part], up_ref[...], NT)
        out_side = mm(g_ref[part], down_ref[...], NT)
        act, slope = gelu_pair(pre)
        low = act.astype(jnp.bfloat16)
        act_ref[part] = low
        product = low.astype(jnp.float32) * out_side
        dots[part] += sum(product[:, k : k + 128] for k in range(0, FT, 128))
        back = (out_side * slope).astype(jnp.bfloat16)
        pre_ref[part] = back
        total[part] += mm(back, up_ref[...], NN)

    @pl.when(step == steps - 1)
    def _():
        back_ref[...] = total[...].astype(jnp.bfloat16)
        dot_ref[...] = lax.dot_general(
            jnp.ones((8, 128), jnp.float32), dots[...], NT,
            precision=HIGHEST, preferred_element_type=jnp.float32)


def expert_first(x, g, up, down):
    rows, width = x.shape
    hidden = up.shape[0]
    steps = hidden // FT
    whole = lambda f: (0, 0)
    return pl.pallas_call(
        functools.partial(expert_kernel, steps),
        grid=(steps,),
        in_specs=[
            pl.BlockSpec((rows, width), whole),
            pl.BlockSpec((rows, width), whole),
            pl.BlockSpec((FT, width), lambda f: (f, 0)),
            pl.BlockSpec((FT, width), lambda f: (f, 0)),
        ],
        out_specs=[
            pl.BlockSpec((rows, FT), lambda f: (0, f)),
            pl.BlockSpec((rows, FT), lambda f: (0, f)),
            pl.BlockSpec((rows, width), whole),
            pl.BlockSpec((8, rows), whole),
        ],
        out_shape=[
            jax.ShapeDtypeStruct((rows, hidden), jnp.bfloat16),
            jax.ShapeDtypeStruct((rows, hidden), jnp.bfloat16),
            jax.ShapeDtypeStruct((rows, width), jnp.bfloat16),
            jax.ShapeDtypeStruct((8, rows), jnp.float32),
        ],
        scratch_shapes=[
            pltpu.VMEM((rows, width), jnp.float32),
            pltpu.VMEM((rows, 128), jnp.float32),
        ],
        compiler_params=pltpu.CompilerParams(vmem_limit_bytes=48 << 20),
        cost_estimate=pl.CostEstimate(
            flops=6 * rows * width * hidden, bytes_accessed=32 << 20, transcendentals=rows * hidden),
        name="expert_first",
    )(x, g, up, down)


def expert_late_kernel(steps, x_ref, g_ref, gate_ref, act_ref, pre_ref, down_ref,
                       out_ref, up_grad_ref, down_grad_ref, total, x_gated, g_gated):
    step = pl.program_id(0)

    @pl.when(step == 0)
    def _():
        total[...] = jnp.zeros_like(total)
        gate = gate_ref[...]
        x_gated[...] = (x_ref[...].astype(jnp.float32) * gate).astype(jnp.bfloat16)
        g_gated[...] = (g_ref[...].astype(jnp.float32) * gate).astype(jnp.bfloat16)

    up_grad_ref[...] = mm(pre_ref[...], x_gated[...], TN).astype(up_grad_ref.dtype)
    down_grad_ref[...] = mm(act_ref[...], g_gated[...], TN).astype(down_grad_ref.dtype)
    total[...] += mm(act_ref[...], down_ref[...], NN)

    @pl.when(step == steps - 1)
    def _():
        out_ref[...] = total[...].astype(jnp.bfloat16)


def expert_late(x, g, gate, act, pre, down):
    rows, width = x.shape
    hidden = down.shape[0]
    steps = hidden // FT
    whole = lambda f: (0, 0)
    tile = pl.BlockSpec((FT, width), lambda f: (f, 0))
    return pl.pallas_call(
        functools.partial(expert_late_kernel, steps),
        grid=(steps,),
        in_specs=[
            pl.BlockSpec((rows, width), whole),
            pl.BlockSpec((rows, width), whole),
            pl.BlockSpec((rows, 1), whole),
            pl.BlockSpec((rows, FT), lambda f: (0, f)),
            pl.BlockSpec((rows, FT), lambda f: (0, f)),
            tile,
        ],
        out_specs=[pl.BlockSpec((rows, width), whole), tile, tile],
        out_shape=[
            jax.ShapeDtypeStruct((rows, width), jnp.bfloat16),
            jax.ShapeDtypeStruct((hidden, width), jnp.bfloat16),
            jax.ShapeDtypeStruct((hidden, width), jnp.bfloat16),
        ],
        scratch_shapes=[
            pltpu.VMEM((rows, width), jnp.float32),
            pltpu.VMEM((rows, width), jnp.bfloat16),
            pltpu.VMEM((rows, width), jnp.bfloat16),
        ],
        compiler_params=pltpu.CompilerParams(vmem_limit_bytes=48 << 20),
        cost_estimate=pl.CostEstimate(
            flops=6 * rows * width * hidden, bytes_accessed=32 << 20, transcendentals=0),
        name="expert_late",
    )(x, g, gate, act, pre, down)


def norm_rows(values, gain):
    return values * lax.rsqrt(jnp.mean(values * values, axis=-1, keepdims=True) + EPSILON) * gain


def norm_back(values, gain, grad):
    r = lax.rsqrt(jnp.mean(values * values, axis=-1, keepdims=True) + EPSILON)
    u = values * r
    du = grad * gain
    return r * (du - u * jnp.mean(du * u, axis=-1, keepdims=True)), grad * u


def body(
    block_input,
    out_grad,
    w_qkv,
    w_out,
    rel_table,
    gain_attn,
    gain_moe,
    w_router,
    w_up,
    w_down,
    routes,
    segments,
    padding,
    rel_bucket,
):
    tensor_pos = lax.axis_index("tensor")
    rows_local, width = block_input.shape
    seq_len = segments.shape[1]
    expert_count = w_router.shape[1]
    capacity = (10 * rows_local + 4 * expert_count - 1) // (4 * expert_count)
    slots = expert_count * capacity
    x_float = block_input.astype(jnp.float32)
    grad_float = out_grad.astype(jnp.float32)

    attn_norm = norm_rows(x_float, gain_attn).astype(jnp.bfloat16)
    seq_rows = lax.all_gather(attn_norm, "tensor", axis=0, tiled=True)
    qkv_full = lax.all_gather(w_qkv, "dp", axis=1, tiled=True)
    out_rows = lax.all_gather(w_out, "dp", axis=1, tiled=True)
    out_full = lax.all_gather(out_rows, "tensor", axis=0, tiled=True)
    up_full = lax.all_gather(w_up[0], "tensor", axis=0, tiled=True)
    down_full = lax.all_gather(w_down[0], "tensor", axis=0, tiled=True)

    live_mask = lax.dynamic_slice_in_dim(padding.reshape(-1), tensor_pos * rows_local, rows_local)
    live_float = live_mask.astype(jnp.float32)
    expert_ids = jnp.arange(expert_count, dtype=jnp.int32)
    pick_first = routes[:, 0:1] == expert_ids[None, :]
    pick_second = routes[:, 1:2] == expert_ids[None, :]
    usable = live_mask[:, None] == 1
    first_hot = (pick_first & usable).astype(jnp.int32)
    second_hot = (pick_second & usable).astype(jnp.int32)
    first_place = jnp.sum((jnp.cumsum(first_hot, axis=0) - first_hot) * first_hot, axis=1)
    second_before = (
        jnp.cumsum(second_hot, axis=0) - second_hot + jnp.sum(first_hot, axis=0, keepdims=True)
    )
    second_place = jnp.sum(second_before * second_hot, axis=1)
    first_slot = jnp.where(
        (live_mask == 1) & (first_place < capacity), routes[:, 0] * capacity + first_place, -1
    )
    second_slot = jnp.where(
        (live_mask == 1) & (second_place < capacity), routes[:, 1] * capacity + second_place, -1
    )
    slot_ids = jnp.arange(slots, dtype=jnp.int32)
    select_first = slot_ids[:, None] == first_slot[None, :]
    select_second = slot_ids[:, None] == second_slot[None, :]
    select_both = (select_first | select_second).astype(jnp.bfloat16)
    select_first_low = select_first.astype(jnp.bfloat16)
    select_second_low = select_second.astype(jnp.bfloat16)

    def to_experts(rows):
        return lax.all_to_all(rows, "dp", split_axis=0, concat_axis=0, tiled=True)

    grad_rows = jnp.dot(select_both, out_grad, preferred_element_type=jnp.float32)
    sent_grads = to_experts(grad_rows.astype(jnp.bfloat16).reshape(expert_count, capacity, width))
    sent_grads = sent_grads.reshape(slots, width)

    heads = qkv_full.shape[2] // DH
    inner = heads * DH
    table_local = lax.dynamic_slice_in_dim(rel_table, tensor_pos * heads, heads, 1)
    bucket_hot = (rel_bucket[:, None] == jnp.arange(NB, dtype=jnp.int32)[None, :]).astype(jnp.float32)
    line = line_of(jnp.dot(bucket_hot, table_local, precision=HIGHEST).T)
    segk, segq = mask_inputs(segments, padding)
    qkv_low, heads_low, lse = attend(line, segk, segq, seq_rows, qkv_full)
    heads_own = lax.all_to_all(heads_low, "tensor", split_axis=0, concat_axis=1, tiled=True)

    middle = x_float + jnp.dot(heads_own, out_full, preferred_element_type=jnp.float32)
    moe_low = norm_rows(middle, gain_moe).astype(jnp.bfloat16)
    rows_out = jnp.dot(select_both, moe_low, preferred_element_type=jnp.float32)
    sent_rows = to_experts(rows_out.astype(jnp.bfloat16).reshape(expert_count, capacity, width))
    sent_rows = sent_rows.reshape(slots, width)
    logits = jnp.dot(moe_low, w_router, preferred_element_type=jnp.float32)
    first_logit = jnp.sum(jnp.where(pick_first, logits, 0.0), axis=1)
    second_logit = jnp.sum(jnp.where(pick_second, logits, 0.0), axis=1)
    first_gate = jax.nn.sigmoid(first_logit - second_logit) * live_float
    second_gate = jax.nn.sigmoid(second_logit - first_logit) * live_float
    slot_gate = jnp.sum(
        jnp.where(select_first, first_gate[None, :], 0.0)
        + jnp.where(select_second, second_gate[None, :], 0.0),
        axis=1,
    )
    sent_gates = to_experts(slot_gate.reshape(expert_count, capacity)).reshape(slots, 1)

    act, pre_grad, back, dots = expert_first(sent_rows, sent_grads, up_full, down_full)
    returned_grad = to_experts(back.reshape(expert_count, capacity, width)).reshape(slots, width)
    slot_dots = to_experts(dots[0].reshape(expert_count, capacity)).reshape(slots)
    produced, up_part, down_part = expert_late(
        sent_rows, sent_grads, sent_gates, act, pre_grad, down_full
    )
    returned = to_experts(produced.reshape(expert_count, capacity, width)).reshape(slots, width)
    w_up_grad = lax.psum_scatter(up_part, "tensor", scatter_dimension=0, tiled=True)
    w_down_grad = lax.psum_scatter(down_part, "tensor", scatter_dimension=0, tiled=True)

    first_dot = jnp.sum(jnp.where(select_first, slot_dots[:, None], 0.0), axis=0)
    second_dot = jnp.sum(jnp.where(select_second, slot_dots[:, None], 0.0), axis=0)
    coefficient = first_gate * second_gate * (first_dot - second_dot)
    logit_grad = (
        jnp.where(pick_first, coefficient[:, None], 0.0)
        - jnp.where(pick_second, coefficient[:, None], 0.0)
    ).astype(jnp.bfloat16)
    router_grad = jnp.einsum("nd,ne->de", moe_low, logit_grad, preferred_element_type=jnp.float32)

    def gated(rows):
        first_rows = jnp.einsum("st,sd->td", select_first_low, rows, preferred_element_type=jnp.float32)
        second_rows = jnp.einsum("st,sd->td", select_second_low, rows, preferred_element_type=jnp.float32)
        return first_gate[:, None] * first_rows + second_gate[:, None] * second_rows

    moe_norm_grad = (
        jnp.einsum("ne,de->nd", logit_grad, w_router, preferred_element_type=jnp.float32)
        + gated(returned_grad)
    )
    middle_back, gain_moe_rows = norm_back(middle, gain_moe, moe_norm_grad)
    middle_grad = grad_float + middle_back
    gain_moe_grad = jnp.sum(gain_moe_rows, axis=0)
    attn_grad = middle_grad.astype(jnp.bfloat16)
    heads_grad = jnp.einsum("nd,fd->nf", attn_grad, out_full, preferred_element_type=jnp.float32)
    heads_grad = lax.all_to_all(
        heads_grad.astype(jnp.bfloat16), "tensor", split_axis=1, concat_axis=0, tiled=True
    )
    out_part = jnp.einsum("nf,nd->fd", heads_own, attn_grad, preferred_element_type=jnp.float32)
    out_part = lax.psum_scatter(out_part.astype(jnp.bfloat16), "tensor", scatter_dimension=0, tiled=True)
    w_out_grad = lax.psum_scatter(out_part.astype(jnp.float32), "dp", scatter_dimension=1, tiled=True)
    gain_moe_grad, router_grad = lax.psum((gain_moe_grad, router_grad), ("dp", "tensor"))

    norm_part, qkv_part, folded = attend_back(
        line, segk, segq, seq_rows, qkv_full, qkv_low, heads_grad, lse
    )
    attn_norm_grad = lax.psum_scatter(norm_part, "tensor", scatter_dimension=0, tiled=True)
    input_back, gain_attn_rows = norm_back(x_float, gain_attn, attn_norm_grad.astype(jnp.float32))
    input_grad = middle_grad + input_back
    gain_attn_grad = jnp.sum(gain_attn_rows, axis=0)
    w_qkv_grad = lax.psum_scatter(qkv_part, "dp", scatter_dimension=1, tiled=True)
    line_grad = lines_of(folded, heads, seq_len // QB)
    table_part = jnp.dot(bucket_hot.T, line_grad.T, precision=HIGHEST)
    table_whole = lax.dynamic_update_slice(
        jnp.zeros(rel_table.shape, jnp.float32), table_part, (0, tensor_pos * heads)
    )
    gain_attn_grad, table_whole = lax.psum((gain_attn_grad, table_whole), ("dp", "tensor"))
    block_output = middle + gated(returned)
    return (
        block_output,
        input_grad,
        w_qkv_grad,
        w_out_grad,
        table_whole,
        gain_attn_grad,
        gain_moe_grad,
        router_grad,
        w_up_grad.astype(jnp.float32)[None],
        w_down_grad.astype(jnp.float32)[None],
    )


def solution(mesh):
    in_specs = (
        P(("dp", "tensor"), None),
        P(("dp", "tensor"), None),
        P(None, "dp", "tensor"),
        P("tensor", "dp"),
        P(),
        P(),
        P(),
        P(),
        P("dp", "tensor", None),
        P("dp", "tensor", None),
        P(("dp", "tensor"), None),
        P("dp", None),
        P("dp", None),
        P(),
    )
    out_specs = (
        P(("dp", "tensor"), None),
        P(("dp", "tensor"), None),
        P(None, "dp", "tensor"),
        P("tensor", "dp"),
        P(),
        P(),
        P(),
        P(),
        P("dp", "tensor", None),
        P("dp", "tensor", None),
    )
    return jax.shard_map(body, mesh=mesh, in_specs=in_specs, out_specs=out_specs, check_vma=False)
```

profile of v0, /device:TPU:0, one launch (start us, length us, event | category | flops | bytes accessed | tf_op | source)
XLA Modules:
  0.0 642.3 jit_solution(10189017074901241615)
XLA Ops:
  11.1 32.9 %all_gather.20 = bf16[192,768]{0,1:T(8,128)(2,1)S(1)} all-gather(bf16[192,96]{0,1:T(8,128)(2,1)S(1)} %copy.54), channel_id=1, replica_groups=mesh['dp'=8,'tensor'=4] {'dp'}, dimensions={1}, use_global_device_ids=true | all-gather | bytes 331776 | tf_op jit(solution)/shard_map/all_gather | solution.py:408
  49.3 34.1 %all_gather.19.w_ref = bf16[3,768,192]{2,1,0:T(8,128)(2,1)S(1)} all-gather(bf16[3,96,192]{2,1,0:T(8,128)(2,1)S(1)} %copy-done.20), channel_id=1, replica_groups=mesh['dp'=8,'tensor'=4] {'dp'}, dimensions={1}, use_global_device_ids=true | all-gather | bytes 995328 | tf_op jit(solution)/shard_map/all_gather | solution.py:407
  87.3 18.4 %attend.1 = (bf16[3,2048,192]{2,1,0:T(8,128)(2,1)}, bf16[2048,192]{1,0:T(8,128)(2,1)S(1)}, f32[2,3,1024]{2,1,0:T(4,128)S(1)}) custom-call(f32[3,1280]{1,0:T(4,128)S(1)} %concatenate.48.line_ref, s32[2,1024,1]{2,1,0:T(8,128)S(1)} %copy-done.4, s32[2,1,1024]{2,1,0:T(1,128)S(1)} %broadcast_in_dim.115.segq_ref, ...), custom_call_target="tpu_custom_call" | custom-call | flops 10000000000 | bytes 10485760 | tf_op jit(solution)/shard_map/attend/pallas_call | solution.py:86
  113.3 17.0 %all-to-all-done = bf16[4,512,192]{1,2,0:T(8,128)(2,1)S(1)} async-done(((bf16[4,512,192]{1,2,0:T(8,128)(2,1)}), bf16[4,512,192]{1,2,0:T(8,128)(2,1)S(1)}, u32[]{:S(2)}, u32[]{:S(2)}) %all-to-all-start) | async-done | bytes 786464 | tf_op jit(solution)/shard_map/all_to_all | solution.py:453
  131.1 5.2 all-to-all-start.2
  144.0 36.8 %all-to-all-done.2 = bf16[8,160,768]{2,1,0:T(8,128)(2,1)S(1)} async-done(((bf16[8,160,768]{2,1,0:T(8,128)(2,1)}), bf16[8,160,768]{2,1,0:T(8,128)(2,1)S(1)}, u32[]{:S(2)}, u32[]{:S(2)}) %all-to-all-start.2) | async-done | bytes 1966112 | tf_op jit(solution)/shard_map/all_to_all | solution.py:440
  180.7 4.3 all-to-all-start.1
  185.1 45.0 %all-to-all-done.1 = bf16[8,160,768]{2,1,0:T(8,128)(2,1)} async-done(((bf16[8,160,768]{2,1,0:T(8,128)(2,1)}), bf16[8,160,768]{2,1,0:T(8,128)(2,1)}, u32[]{:S(2)}, u32[]{:S(2)}) %all-to-all-start.1) | async-done | bytes 1966112 | tf_op jit(solution)/shard_map/all_to_all | solution.py:440
  230.1 30.4 %expert_first.1 = (bf16[1280,3072]{1,0:T(8,128)(2,1)}, bf16[1280,3072]{1,0:T(8,128)(2,1)}, bf16[1280,768]{1,0:T(8,128)(2,1)S(1)}, f32[8,1280]{1,0:T(8,128)S(1)}) custom-call(bf16[1280,768]{1,0:T(8,128)(2,1)} %bitcast.14.x_ref, bf16[1280,768]{1,0:T(8,128)(2,1)S(1)} %bitcast.102, bf16[3072,768]{1,0:T(8,128)(2,1)} %bitcast.150, bf16[3072,768]{1,0:T(8,128)(2,1)} %bitcast.148), custom_call_target="tpu_custom_call" | custom-call | flops 18119393280 | bytes 33554432 | tf_op jit(solution)/shard_map/expert_first/pallas_call | solution.py:282
  261.9 9.9 %all_to_all.77 = f32[8,1,160]{2,1,0:T(1,128)S(1)} all-to-all(f32[8,1,160]{2,1,0:T(1,128)S(1)} %all_to_all.68), channel_id=1, replica_groups=mesh['dp'=8,'tensor'=4] {'dp'}, dimensions={0} | all-to-all | bytes 10240 | tf_op jit(solution)/shard_map/all_to_all | solution.py:440
  271.8 4.5 all-to-all-start.6
  278.9 41.8 %all-to-all-done.6 = bf16[8,160,768]{2,1,0:T(8,128)(2,1)} async-done(((bf16[8,160,768]{2,1,0:T(8,128)(2,1)}), bf16[8,160,768]{2,1,0:T(8,128)(2,1)}, u32[]{:S(2)}, u32[]{:S(2)}) %all-to-all-start.6) | async-done | bytes 1966112 | tf_op jit(solution)/shard_map/all_to_all | solution.py:440
  323.8 3.5 multiply_reduce_fusion
  330.9 9.9 %all_to_all.78 = f32[8,1,160]{2,1,0:T(1,128)S(1)} all-to-all(f32[8,1,160]{2,1,0:T(1,128)S(1)} %all_to_all.58), channel_id=1, replica_groups=mesh['dp'=8,'tensor'=4] {'dp'}, dimensions={0} | all-to-all | bytes 10240 | tf_op jit(solution)/shard_map/all_to_all | solution.py:440
  341.3 13.5 %reduce-scatter.13.cloned.1.call-done = bf16[192,768]{1,0:T(8,128)(2,1)} async-done(((bf16[768,768]{1,0:T(8,128)(2,1)}), bf16[192,768]{1,0:T(8,128)(2,1)}) %reduce-scatter.13.cloned.1.call-update) | async-done | bytes 294928 | tf_op jit(solution)/shard_map/reduce_scatter | solution.py:509
  356.9 26.3 %expert_late.1 = (bf16[1280,768]{1,0:T(8,128)(2,1)}, bf16[3072,768]{1,0:T(8,128)(2,1)}, bf16[3072,768]{1,0:T(8,128)(2,1)}) custom-call(bf16[1280,768]{1,0:T(8,128)(2,1)} %bitcast.14.x_ref, bf16[1280,768]{1,0:T(8,128)(2,1)} %bitcast.103, f32[1280,1]{1,0:T(8,128)S(1)} %reshape.172.gate_ref, bf16[1280,3072]{1,0:T(8,128)(2,1)} %get-tuple-element.24.act_ref, ...), custom_call_target="tpu_custom_call" | custom-call | flops 18119393280 | bytes 33554432 | tf_op jit(solution)/shard_map/expert_late/pallas_call | solution.py:340
  389.1 14.1 %all_to_all.79 = bf16[512,4,192]{0,2,1:T(8,128)(2,1)S(1)} all-to-all(bf16[512,4,192]{0,2,1:T(8,128)(2,1)S(1)} %bitcast.111), channel_id=1, replica_groups=mesh['dp'=8,'tensor'=4] {'tensor'}, dimensions={1} | all-to-all | bytes 1572864 | tf_op jit(solution)/shard_map/all_to_all | solution.py:505
  404.9 28.1 %attend_back.1 = (bf16[2048,768]{1,0:T(8,128)(2,1)}, f32[3,768,192]{2,1,0:T(8,128)}, f32[12,8,512]{2,1,0:T(8,128)S(1)}) custom-call(f32[3,1280]{1,0:T(4,128)S(1)} %concatenate.48.line_ref, s32[2,1024,1]{2,1,0:T(8,128)S(1)} %copy-done.5, s32[2,1,1024]{2,1,0:T(1,128)S(1)} %broadcast_in_dim.115.segq_ref, ...), custom_call_target="tpu_custom_call" | custom-call | flops 20000000000 | bytes 16777216 | tf_op jit(solution)/shard_map/attend_back/pallas_call | solution.py:189
  433.0 5.7 all-to-all-start.4
  438.9 45.2 %all-to-all-done.4 = bf16[8,160,768]{2,1,0:T(8,128)(2,1)S(1)} async-done(((bf16[8,160,768]{2,1,0:T(8,128)(2,1)}), bf16[8,160,768]{2,1,0:T(8,128)(2,1)S(1)}, u32[]{:S(2)}, u32[]{:S(2)}) %all-to-all-start.4) | async-done | bytes 1966112 | tf_op jit(solution)/shard_map/all_to_all | solution.py:440
  495.1 25.6 %reduce-scatter.15.cloned.1.call-done = bf16[768,768]{1,0:T(8,128)(2,1)} async-done(((bf16[3072,768]{1,0:T(8,128)(2,1)}), bf16[768,768]{1,0:T(8,128)(2,1)}) %reduce-scatter.15.cloned.1.call-update) | async-done | bytes 1179664 | tf_op jit(solution)/shard_map/reduce_scatter | solution.py:479
  523.6 37.7 %reduce-scatter.9.cloned.1.call-done = bf16[512,768]{1,0:T(8,128)(2,1)} async-done(((bf16[2048,768]{1,0:T(8,128)(2,1)}), bf16[512,768]{1,0:T(8,128)(2,1)}) %reduce-scatter.9.cloned.1.call-update) | async-done | bytes 786448 | tf_op jit(solution)/shard_map/reduce_scatter | solution.py:516
  563.1 41.9 %all-reduce.2 = (f32[32,12]{0,1:T(8,128)}, f32[768]{0:T(1024)}, f32[768]{0:T(1024)}, f32[768,8]{0,1:T(8,128)}) all-reduce(f32[32,12]{0,1:T(8,128)S(1)} %dynamic_update_slice.3, f32[768]{0:T(1024)S(1)} %get-tuple-element.38, f32[768]{0:T(1024)S(1)} %get-tuple-element.36, ...), channel_id=1, replica_groups=mesh['dp'=8,'tensor'=4] {'dp','tensor'}, use_global_device_ids=true, to_apply=%region_20.21 | all-reduce | flops 8064 | bytes 64512 | tf_op jit(solution)/shard_map/psum | solution.py:526
  607.8 27.2 %reduce-scatter.11.cloned.1.call-done = f32[3,96,192]{2,1,0:T(8,128)} async-done(((f32[3,768,192]{2,1,0:T(8,128)}), f32[3,96,192]{2,1,0:T(8,128)}) %reduce-scatter.11.cloned.1.call-update) | async-done | bytes 221200 | tf_op jit(solution)/shard_map/reduce_scatter | solution.py:520
  (190 shorter events, 68.1 us)
Async XLA Ops:
  7.2 269.3 %copy-start = (bf16[768,8]{0,1:T(8,128)(2,1)S(1)}, bf16[768,8]{0,1:T(8,128)(2,1)}, u32[]{:S(2)}) copy-start(bf16[768,8]{0,1:T(8,128)(2,1)} %param.21) | copy-start | bytes 36868
  7.2 78.9 %all-gather.7.cloned.1.call-start = ((), (), s32[]{:S(2)}) async-start(), calls=%async_computation.14 | async-start | bytes 3932160 | tf_op jit(solution)/shard_map/all_gather | solution.py:406
  10.9 125.5 %all-gather.9.cloned.1.call-start = ((), (), s32[]{:S(2)}) async-start(), calls=%async_computation.15 | async-start | bytes 1474560 | tf_op jit(solution)/shard_map/all_gather | solution.py:409
  44.9 140.2 %all-gather.13.cloned.1.call-start = ((), (), s32[]{:S(2)}) async-start(), calls=%async_computation.22 | async-start | bytes 5898240 | tf_op jit(solution)/shard_map/all_gather | solution.py:411
  45.6 139.5 %all-gather.11.cloned.1.call-start = ((), (), s32[]{:S(2)}) async-start(), calls=%async_computation.21 | async-start | bytes 5898240 | tf_op jit(solution)/shard_map/all_gather | solution.py:410
  46.2 38.6 %copy-start.28 = (s32[1024]{0:T(1024)S(1)}, s32[1024]{0:T(1024)}, u32[]{:S(2)}) copy-start(s32[1024]{0:T(1024)} %param.27) | copy-start | bytes 12292
  49.3 56.4 %copy-start.26 = (s32[8,5]{0,1:T(8,128)}, s32[8,5]{0,1:T(8,128)S(1)}, u32[]{:S(2)}) copy-start(s32[8,5]{0,1:T(8,128)S(1)} %reduce-window.19) | copy-start | bytes 484
  107.0 23.3 %all-to-all-start = ((bf16[4,512,192]{1,2,0:T(8,128)(2,1)}), bf16[4,512,192]{1,2,0:T(8,128)(2,1)S(1)}, u32[]{:S(2)}, u32[]{:S(2)}) async-start(bf16[4,512,192]{1,2,0:T(8,128)(2,1)} %copy.53), calls=%async_computation | async-start | bytes 1572864 | tf_op jit(solution)/shard_map/all_to_all | solution.py:453
  131.1 49.6 %all-to-all-start.2 = ((bf16[8,160,768]{2,1,0:T(8,128)(2,1)}), bf16[8,160,768]{2,1,0:T(8,128)(2,1)S(1)}, u32[]{:S(2)}, u32[]{:S(2)}) async-start(bf16[8,160,768]{2,1,0:T(8,128)(2,1)} %bitcast.114), calls=%async_computation.2 | async-start | bytes 3932160 | tf_op jit(solution)/shard_map/all_to_all | solution.py:440
  180.7 49.4 %copy-start.2 = (bf16[8,160,768]{2,1,0:T(8,128)(2,1)}, bf16[8,160,768]{2,1,0:T(8,128)(2,1)S(1)}, u32[]{:S(2)}) copy-start(bf16[8,160,768]{2,1,0:T(8,128)(2,1)S(1)} %all-to-all-done.2) | copy-start | bytes 5898244
  180.7 49.4 %all-to-all-start.1 = ((bf16[8,160,768]{2,1,0:T(8,128)(2,1)}), bf16[8,160,768]{2,1,0:T(8,128)(2,1)}, u32[]{:S(2)}, u32[]{:S(2)}) async-start(bf16[8,160,768]{2,1,0:T(8,128)(2,1)} %bitcast.115), calls=%async_computation.1 | async-start | bytes 3932160 | tf_op jit(solution)/shard_map/all_to_all | solution.py:440
  271.8 48.9 %all-to-all-start.6 = ((bf16[8,160,768]{2,1,0:T(8,128)(2,1)}), bf16[8,160,768]{2,1,0:T(8,128)(2,1)}, u32[]{:S(2)}, u32[]{:S(2)}) async-start(bf16[8,160,768]{2,1,0:T(8,128)(2,1)} %bitcast.104), calls=%async_computation.6 | async-start | bytes 3932160 | tf_op jit(solution)/shard_map/all_to_all | solution.py:440
  276.3 78.5 %reduce-scatter.13.cloned.1.call-start = ((), (), s32[]{:S(2)}) async-start(), calls=%async_computation.18 | async-start | bytes 1474560 | tf_op jit(solution)/shard_map/reduce_scatter | solution.py:509
  330.7 159.7 %reduce-scatter.19.cloned.1.call-start = ((), (), s32[]{:S(2)}) async-start(), calls=%async_computation.23 | async-start | bytes 884736
  356.8 135.3 %reduce-scatter.17.cloned.1.call-start = ((), (), s32[]{:S(2)}) async-start(), calls=%async_computation.20 | async-start | bytes 5898240 | tf_op jit(solution)/shard_map/reduce_scatter | solution.py:480
  383.2 137.6 %reduce-scatter.15.cloned.1.call-start = ((), (), s32[]{:S(2)}) async-start(), calls=%async_computation.19 | async-start | bytes 5898240 | tf_op jit(solution)/shard_map/reduce_scatter | solution.py:479
  383.9 177.4 %reduce-scatter.9.cloned.1.call-start = ((), (), s32[]{:S(2)}) async-start(), calls=%async_computation.16 | async-start | bytes 3932160 | tf_op jit(solution)/shard_map/reduce_scatter | solution.py:516
  432.9 5.7 copy-start.12
  433.0 51.1 %all-to-all-start.4 = ((bf16[8,160,768]{2,1,0:T(8,128)(2,1)}), bf16[8,160,768]{2,1,0:T(8,128)(2,1)S(1)}, u32[]{:S(2)}, u32[]{:S(2)}) async-start(bf16[8,160,768]{2,1,0:T(8,128)(2,1)} %bitcast.19), calls=%async_computation.4 | async-start | bytes 3932160 | tf_op jit(solution)/shard_map/all_to_all | solution.py:440
  438.6 196.4 %reduce-scatter.11.cloned.1.call-start = ((), (), s32[]{:S(2)}) async-start(), calls=%async_computation.17 | async-start | bytes 2654208 | tf_op jit(solution)/shard_map/reduce_scatter | solution.py:520
  495.1 66.2 %copy-start.9 = (bf16[512,768]{1,0:T(8,128)(2,1)S(1)}, bf16[512,768]{1,0:T(8,128)(2,1)}, u32[]{:S(2)}) copy-start(bf16[512,768]{1,0:T(8,128)(2,1)} %param.14) | copy-start | bytes 2359300
  495.1 66.2 %copy-start.22 = (f32[768]{0:T(1024)S(1)}, f32[768]{0:T(1024)}, u32[]{:S(2)}) copy-start(f32[768]{0:T(1024)} %param.19) | copy-start | bytes 9220
  523.6 81.4 %copy-start.8 = (f32[512,768]{1,0:T(8,128)S(1)}, f32[512,768]{1,0:T(8,128)}, u32[]{:S(2)}) copy-start(f32[512,768]{1,0:T(8,128)} %copy-done.6) | copy-start | bytes 4718596
  605.0 30.0 %copy-start.1 = (bf16[768,8]{0,1:T(8,128)(2,1)S(1)}, bf16[768,8]{0,1:T(8,128)(2,1)}, u32[]{:S(2)}) copy-start(bf16[768,8]{0,1:T(8,128)(2,1)} %param.21) | copy-start | bytes 36868
  (21 other events, 52.4 us)
Sparse Core Ops, SparseCore 0:
  11.0 31.2 all-gather.6
  45.0 18.3 all-gather.8
  65.0 37.4 all-gather.12
  103.9 45.0 all-gather.10
  330.8 23.8 reduce-scatter.12
  358.3 62.4 reduce-scatter.18
  423.3 46.7 reduce-scatter.16
  472.9 47.8 reduce-scatter.14
  523.3 37.9 reduce-scatter.8
  565.6 69.3 reduce-scatter.10
where the time goes:
time: 651 us; the launch traced here: 642 us
  waiting for transfers between devices  292 us (45%)
  blocking collectives  143 us (22%)
  Pallas kernels  103 us (16%)
  matrix products  25.7 us (4%)
  starting transfers between devices  23.9 us (4%)
  local copies, waits for them, and re-layouts  20 us (3%)
  other arithmetic  19.7 us (3%)
  between operations  15.2 us (2%)
    all_to_all x4, waiting for transfers between devices, to_experts(): return lax.all_to_all(rows, 'dp', split_axis=0, concat_axis=0, tiled=True)  169 us
    psum x1, blocking collectives, body(): lax.psum((gain_attn_grad, table_whole), ('dp', 'tensor'))  41.9 us
    reduce_scatter x1, waiting for transfers between devices, body(): lax.psum_scatter(norm_part, 'tensor', scatter_dimension=0, tiled=True)  37.7 us
    all_gather x1, blocking collectives, body(): qkv_full = lax.all_gather(w_qkv, 'dp', axis=1, tiled=True)  34.1 us
    all_gather x1, blocking collectives, body(): out_rows = lax.all_gather(w_out, 'dp', axis=1, tiled=True)  32.9 us
    pallas_call x1, Pallas kernels, expert_first(): pl.pallas_call(functools.partial(expert_kernel, steps), grid=(steps,), in...  30.4 us
    pallas_call x1, Pallas kernels, attend_back(): pl.pallas_call(functools.partial(attend_back_kernel, heads, blocks, seqs)...  28.1 us
    reduce_scatter x1, waiting for transfers between devices, body(): lax.psum_scatter(qkv_part, 'dp', scatter_dimension=1, tiled=True)  27.2 us
  transfers between devices with their start and end apart: 15, of which 9 were waited for; matrix products, arithmetic and copies ran while one was open for 7% of the time, Pallas kernels for 11%

commit v1 on v0

--- a/solution.py
+++ b/solution.py
@@ -34,10 +34,10 @@
 
 def score_block(keys, query, tiles, h, qb, segk_ref, segq_ref):
     raw = mm(keys, query, NT)
-    q_seg = segq_ref[0, :, qb * QB : (qb + 1) * QB]
+    q_seg = segq_ref[:, qb * QB : (qb + 1) * QB]
     parts = []
     for kb in range(qb + 1):
-        k_seg = segk_ref[0, kb * QB : (kb + 1) * QB, :]
+        k_seg = segk_ref[kb * QB : (kb + 1) * QB, :]
         same = k_seg == q_seg
         if kb == qb:
             row = lax.broadcasted_iota(jnp.int32, (QB, QB), 0)
@@ -49,67 +49,6 @@
     return parts
 
 
-def attend_kernel(heads, blocks, line_ref, segk_ref, segq_ref, rows_ref, w_ref,
-                  qkv_ref, out_ref, lse_ref, tiles):
-    @pl.when(pl.program_id(0) == 0)
-    def _():
-        build_bias(line_ref, tiles, heads, blocks)
-
-    for c in range(3):
-        qkv_ref[c] = mm(rows_ref[...], w_ref[c], NN).astype(jnp.bfloat16)
-    scale = 1.0 / math.sqrt(DH)
-    for qb in range(blocks):
-        nk = (qb + 1) * QB
-        lower = qb * QB
-        turned = []
-        for h in range(heads):
-            cols = slice(h * DH, (h + 1) * DH)
-            query = (qkv_ref[0, lower : lower + QB, cols].astype(jnp.float32) * scale).astype(jnp.bfloat16)
-            parts = score_block(qkv_ref[1, 0:nk, cols], query, tiles, h, qb, segk_ref, segq_ref)
-            peak = functools.reduce(jnp.maximum, [jnp.max(x, axis=0, keepdims=True) for x in parts])
-            probs = [jnp.exp(x - peak) for x in parts]
-            total = functools.reduce(jnp.add, [jnp.sum(x, axis=0, keepdims=True) for x in probs])
-            mixed = functools.reduce(jnp.add, [
-                mm(qkv_ref[2, kb * QB : (kb + 1) * QB, cols], x.astype(jnp.bfloat16), TN)
-                for kb, x in enumerate(probs)])
-            turned.append(mixed / total)
-            lse_ref[0, h : h + 1, lower : lower + QB] = peak + jnp.log(total)
-        out_ref[lower : lower + QB, :] = jnp.concatenate(turned, axis=0).T.astype(jnp.bfloat16)
-
-
-def attend(line, segk, segq, rows, w):
-    seqs, _, seq_len = segq.shape
-    heads = line.shape[0]
-    inner = heads * DH
-    blocks = seq_len // QB
-    width = rows.shape[1]
-    return pl.pallas_call(
-        functools.partial(attend_kernel, heads, blocks),
-        grid=(seqs,),
-        in_specs=[
-            pl.BlockSpec(line.shape, lambda s: (0, 0)),
-            pl.BlockSpec((1, seq_len, 1), lambda s: (s, 0, 0)),
-            pl.BlockSpec((1, 1, seq_len), lambda s: (s, 0, 0)),
-            pl.BlockSpec((seq_len, width), lambda s: (s, 0)),
-            pl.BlockSpec(w.shape, lambda s: (0, 0, 0)),
-        ],
-        out_specs=[
-            pl.BlockSpec((3, seq_len, inner), lambda s: (0, s, 0)),
-            pl.BlockSpec((seq_len, inner), lambda s: (s, 0)),
-            pl.BlockSpec((1, heads, seq_len), lambda s: (s, 0, 0)),
-        ],
-        out_shape=[
-            jax.ShapeDtypeStruct((3, seqs * seq_len, inner), jnp.bfloat16),
-            jax.ShapeDtypeStruct((seqs * seq_len, inner), jnp.bfloat16),
-            jax.ShapeDtypeStruct((seqs, heads, seq_len), jnp.float32),
-        ],
-        scratch_shapes=[pltpu.VMEM((heads, blocks, QB, QB), jnp.float32)],
-        compiler_params=pltpu.CompilerParams(vmem_limit_bytes=48 << 20),
-        cost_estimate=pl.CostEstimate(flops=10_000_000_000, bytes_accessed=10 << 20, transcendentals=4_000_000),
-        name="attend",
-    )(line, segk, segq, rows, w)
-
-
 def attend_back_kernel(heads, blocks, seqs, line_ref, segk_ref, segq_ref, rows_ref, w_ref,
                        qkv_ref, og_ref, lse_ref,
                        norm_ref, wg_ref, lg_ref, tiles, sums, kg, vg, dq):
@@ -129,12 +68,12 @@
         for qb in range(blocks):
             nk = (qb + 1) * QB
             lower = qb * QB
-            query = (qkv_ref[0, lower : lower + QB, cols].astype(jnp.float32) * scale).astype(jnp.bfloat16)
+            query = (qkv_ref[0, 0, lower : lower + QB, cols].astype(jnp.float32) * scale).astype(jnp.bfloat16)
             grad = og_ref[lower : lower + QB, cols]
             lse = lse_ref[0, h : h + 1, lower : lower + QB]
-            parts = score_block(qkv_ref[1, 0:nk, cols], query, tiles, h, qb, segk_ref, segq_ref)
+            parts = score_block(qkv_ref[0, 1, 0:nk, cols], query, tiles, h, qb, segk_ref.at[0], segq_ref.at[0])
             probs = [jnp.exp(x - lse) for x in parts]
-            pg = mm(qkv_ref[2, 0:nk, cols], grad, NT)
+            pg = mm(qkv_ref[0, 2, 0:nk, cols], grad, NT)
             pgs = [pg[kb * QB : (kb + 1) * QB] for kb in range(qb + 1)]
             delta = functools.reduce(jnp.add, [jnp.sum(p * g, axis=0, keepdims=True) for p, g in zip(probs, pgs)])
             dqt = jnp.zeros((DH, QB), jnp.float32)
@@ -144,7 +83,7 @@
                 sums[h, qb - kb] += sg.astype(jnp.float32)
                 vg[rows] += mm(probs[kb].astype(jnp.bfloat16), grad, NN)
                 kg[rows] += mm(sg, query, NN)
-                dqt = dqt + mm(qkv_ref[1, rows, cols], sg, TN)
+                dqt = dqt + mm(qkv_ref[0, 1, rows, cols], sg, TN)
             dq[lower : lower + QB, h * DH : (h + 1) * DH] = (dqt * scale).T.astype(jnp.bfloat16)
         inner = heads * DH
         dq[:, inner + h * DH : inner + (h + 1) * DH] = kg[...].astype(jnp.bfloat16)
@@ -195,7 +134,7 @@
             pl.BlockSpec((1, 1, seq_len), lambda s: (s, 0, 0)),
             pl.BlockSpec((seq_len, width), lambda s: (s, 0)),
             pl.BlockSpec(w.shape, lambda s: (0, 0, 0)),
-            pl.BlockSpec((3, seq_len, inner), lambda s: (0, s, 0)),
+            pl.BlockSpec((1, 3, seq_len, inner), lambda s: (s, 0, 0, 0)),
             pl.BlockSpec((seq_len, inner), lambda s: (s, 0)),
             pl.BlockSpec((1, heads, seq_len), lambda s: (s, 0, 0)),
         ],
@@ -229,6 +168,222 @@
 
 def line_of(by_distance):
     return jnp.concatenate([jnp.full((by_distance.shape[0], QB), NEGATIVE, jnp.float32), by_distance], axis=1)
+
+
+MESH = pl.DeviceIdType.MESH
+
+
+def remote(src, dst, send, recv, axis, place):
+    return pltpu.make_async_remote_copy(
+        src_ref=src, dst_ref=dst, send_sem=send, recv_sem=recv, device_id={axis: place}, device_id_type=MESH
+    )
+
+
+def each_peer(count, step):
+    if count <= 8:
+        for r in range(1, count):
+            step(r)
+    else:
+        def one(r, carry):
+            step(r)
+            return carry
+        lax.fori_loop(1, count, one, 0)
+
+
+def greet(dp_count, tensor_count):
+    barrier = pltpu.get_barrier_semaphore()
+    dp, tp = lax.axis_index("dp"), lax.axis_index("tensor")
+    for r in range(1, tensor_count):
+        pl.semaphore_signal(barrier, inc=1, device_id={"tensor": lax.rem(tp + r, tensor_count)}, device_id_type=MESH)
+
+    def signal(r):
+        pl.semaphore_signal(barrier, inc=1, device_id={"dp": lax.rem(dp + r, dp_count)}, device_id_type=MESH)
+    each_peer(dp_count, signal)
+    return lambda: pl.semaphore_wait(barrier, tensor_count - 1 + dp_count - 1)
+
+
+def place_pairs(routes_ref, live_ref, experts, capacity, cap_rows):
+    tokens = live_ref.shape[1]
+    live = live_ref[...] == 1
+    ids = lax.broadcasted_iota(jnp.int32, (experts, tokens), 0)
+    row = lax.broadcasted_iota(jnp.int32, (tokens, tokens), 0)
+    col = lax.broadcasted_iota(jnp.int32, (tokens, tokens), 1)
+    before = (row < col).astype(jnp.float32).astype(jnp.bfloat16)
+    slots = []
+    base = jnp.zeros((experts, 1), jnp.float32)
+    for k in range(2):
+        route = routes_ref[k : k + 1, :]
+        hot = jnp.where((ids == route) & live, 1.0, 0.0)
+        count = mm(hot.astype(jnp.bfloat16), before, NN) + base
+        place = jnp.sum(count * hot, axis=0, keepdims=True).astype(jnp.int32)
+        slots.append(jnp.where(live & (place < capacity), route * cap_rows + place, -1))
+        base = base + jnp.sum(hot, axis=1, keepdims=True)
+    return slots
+
+
+def chosen(first, second, expert, cap_rows):
+    ids = lax.broadcasted_iota(jnp.int32, (cap_rows, first.shape[1]), 0) + expert * cap_rows
+    return jnp.where((ids == first) | (ids == second), 1.0, 0.0).astype(jnp.bfloat16)
+
+
+def attend_sequence(heads, blocks, seq, line_tiles, segk_ref, segq_ref, qkv, heads_out, lse_ref):
+    scale = 1.0 / math.sqrt(DH)
+    for qb in range(blocks):
+        nk = (qb + 1) * QB
+        lower = qb * QB
+        turned = []
+        for h in range(heads):
+            cols = slice(h * DH, (h + 1) * DH)
+            query = (qkv[seq, 0, lower : lower + QB, cols].astype(jnp.float32) * scale).astype(jnp.bfloat16)
+            parts = score_block(qkv[seq, 1, 0:nk, cols], query, line_tiles, h, qb, segk_ref.at[seq], segq_ref.at[seq])
+            peak = functools.reduce(jnp.maximum, [jnp.max(x, axis=0, keepdims=True) for x in parts])
+            probs = [jnp.exp(x - peak) for x in parts]
+            total = functools.reduce(jnp.add, [jnp.sum(x, axis=0, keepdims=True) for x in probs])
+            mixed = functools.reduce(jnp.add, [
+                mm(qkv[seq, 2, kb * QB : (kb + 1) * QB, cols], x.astype(jnp.bfloat16), TN)
+                for kb, x in enumerate(probs)])
+            turned.append(mixed / total)
+            lse_ref[seq, h : h + 1, lower : lower + QB] = peak + jnp.log(total)
+        mixed = jnp.concatenate(turned, axis=0).T.astype(jnp.bfloat16)
+        half = blocks // 2
+        heads_out[seq * 2 + qb // half, (qb % half) * QB : (qb % half + 1) * QB, :] = mixed
+
+
+def front_kernel(sizes, x_ref, gain_ref, w_ref, grad_ref, routes_ref, live_ref, line_ref, segk_ref, segq_ref,
+                 rows, w_all, qkv, lse_ref, heads_all, slots_ref, cot,
+                 tiles, heads_out, cot_send,
+                 far_send, far_recv, w_send, w_recv, cot_s, cot_r, head_send, head_recv, local_sem):
+    dp_count, tensor_count, experts, capacity, cap_rows, heads, blocks, gather_w = sizes
+    dp, tp = lax.axis_index("dp"), lax.axis_index("tensor")
+    sib, opp = tp + 1 - 2 * lax.rem(tp, 2), lax.rem(tp + 2, tensor_count)
+    wait_barrier = greet(dp_count, tensor_count)
+
+    x = x_ref[...].astype(jnp.float32)
+    r = lax.rsqrt(jnp.mean(x * x, axis=-1, keepdims=True) + EPSILON)
+    rows[tp] = (x * r * gain_ref[...]).astype(jnp.bfloat16)
+    wait_barrier()
+
+    half = rows.shape[1] // 2
+    parts = [pl.ds(0, half), pl.ds(half, half)]
+    far = [remote(rows.at[tp, p], rows.at[tp, p], far_send.at[k], far_recv.at[k], "tensor", opp) for k, p in enumerate(parts)]
+    near = remote(rows.at[tp], rows.at[tp], far_send.at[2], far_recv.at[2], "tensor", sib)
+    onward = [remote(rows.at[opp, p], rows.at[opp, p], far_send.at[3 + k], far_recv.at[3 + k], "tensor", sib) for k, p in enumerate(parts)]
+    for c in far:
+        c.start()
+    near.start()
+
+    def w_copy(r):
+        return remote(w_ref, w_all.at[:, dp], w_send.at[r], w_recv.at[r], "dp", lax.rem(dp + r, dp_count))
+    if gather_w:
+        each_peer(dp_count, lambda r: w_copy(r).start())
+        own_w = pltpu.make_async_copy(w_ref, w_all.at[:, dp], local_sem.at[0])
+        own_w.start()
+
+    first, second = place_pairs(routes_ref, live_ref, experts, capacity, cap_rows)
+    slots_ref[0:1, :] = first
+    slots_ref[1:2, :] = second
+
+    def cot_copy(r):
+        to = lax.rem(dp + r, dp_count)
+        return remote(cot_send.at[to], cot.at[dp], cot_s.at[r], cot_r.at[r], "dp", to)
+
+    def cot_fill(r):
+        to = lax.rem(dp + r, dp_count)
+        cot_send[to] = mm(chosen(first, second, to, cap_rows), grad_ref[...], NN).astype(jnp.bfloat16)
+
+    def cot_go(r):
+        cot_fill(r)
+        cot_copy(r).start()
+    each_peer(dp_count, cot_go)
+    cot_fill(0)
+    own_cot = pltpu.make_async_copy(cot_send.at[dp], cot.at[dp], local_sem.at[1])
+    own_cot.start()
+
+    build_bias(line_ref, tiles, heads, blocks)
+    if gather_w:
+        own_w.wait()
+        each_peer(dp_count, lambda r: w_copy(r).wait_recv())
+    near.wait_recv()
+
+    width = rows.shape[2]
+    own_seq = tp // 2
+    inner = heads * DH
+
+    def project(seq):
+        tokens = rows[pl.ds(seq * 2, 2)].reshape(2 * rows.shape[1], width)
+        for c in range(3):
+            weight = w_all[c].reshape(width, inner) if gather_w else w_ref[c]
+            qkv[seq, c] = mm(tokens, weight, NN).astype(jnp.bfloat16)
+
+    def head_copy(k, to):
+        return remote(heads_out.at[to], heads_all.at[tp], head_send.at[k], head_recv.at[k], "tensor", to)
+
+    project(own_seq)
+    for k in range(2):
+        far[k].wait_recv()
+        onward[k].start()
+    attend_sequence(heads, blocks, own_seq, tiles, segk_ref, segq_ref, qkv, heads_out, lse_ref)
+    head_copy(0, sib).start()
+    heads_all[tp] = heads_out[tp]
+    for k in range(2):
+        onward[k].wait_recv()
+    other = 1 - own_seq
+    project(other)
+    attend_sequence(heads, blocks, other, tiles, segk_ref, segq_ref, qkv, heads_out, lse_ref)
+    across = lax.rem(sib + 2, tensor_count)
+    head_copy(1, opp).start()
+    head_copy(2, across).start()
+
+    own_cot.wait()
+    each_peer(dp_count, lambda r: cot_copy(r).wait())
+    if gather_w:
+        each_peer(dp_count, lambda r: w_copy(r).wait_send())
+    for c in far + [near] + onward:
+        c.wait_send()
+    head_copy(0, sib).wait()
+    head_copy(1, opp).wait()
+    head_copy(2, across).wait()
+
+
+def front(sizes, x, gain, w, grad, routes_t, live_row, line, segk, segq):
+    dp_count, tensor_count, experts, capacity, cap_rows, heads, blocks, gather_w = sizes
+    tokens, width = x.shape
+    seq_len = blocks * QB
+    seqs = tensor_count * tokens // seq_len
+    inner = heads * DH
+    vmem = pl.BlockSpec(memory_space=pltpu.VMEM)
+    return pl.pallas_call(
+        functools.partial(front_kernel, sizes),
+        in_specs=[vmem] * 9,
+        out_specs=[vmem] * 7,
+        out_shape=[
+            jax.ShapeDtypeStruct((tensor_count, tokens, width), jnp.bfloat16),
+            jax.ShapeDtypeStruct((3, dp_count, width // dp_count, inner) if gather_w else (3, 8, 128), jnp.bfloat16),
+            jax.ShapeDtypeStruct((seqs, 3, seq_len, inner), jnp.bfloat16),
+            jax.ShapeDtypeStruct((seqs, heads, seq_len), jnp.float32),
+            jax.ShapeDtypeStruct((tensor_count, tokens, inner), jnp.bfloat16),
+            jax.ShapeDtypeStruct((8, tokens), jnp.int32),
+            jax.ShapeDtypeStruct((experts, cap_rows, width), jnp.bfloat16),
+        ],
+        scratch_shapes=[
+            pltpu.VMEM((heads, blocks, QB, QB), jnp.float32),
+            pltpu.VMEM((tensor_count, tokens, inner), jnp.bfloat16),
+            pltpu.VMEM((experts, cap_rows, width), jnp.bfloat16),
+            pltpu.SemaphoreType.DMA((5,)),
+            pltpu.SemaphoreType.DMA((5,)),
+            pltpu.SemaphoreType.DMA((dp_count,)),
+            pltpu.SemaphoreType.DMA((dp_count,)),
+            pltpu.SemaphoreType.DMA((dp_count,)),
+            pltpu.SemaphoreType.DMA((dp_count,)),
+            pltpu.SemaphoreType.DMA((3,)),
+            pltpu.SemaphoreType.DMA((3,)),
+            pltpu.SemaphoreType.DMA((2,)),
+        ],
+        compiler_params=pltpu.CompilerParams(
+            vmem_limit_bytes=56 << 20, collective_id=1, has_side_effects=True),
+        cost_estimate=pl.CostEstimate(flops=20_000_000_000, bytes_accessed=20 << 20, transcendentals=4_000_000),
+        name="front",
+    )(x, gain, w, grad, routes_t, live_row, line, segk, segq)
 
 
 FT = 512
@@ -398,13 +553,16 @@
     seq_len = segments.shape[1]
     expert_count = w_router.shape[1]
     capacity = (10 * rows_local + 4 * expert_count - 1) // (4 * expert_count)
-    slots = expert_count * capacity
     x_float = block_input.astype(jnp.float32)
     grad_float = out_grad.astype(jnp.float32)
 
-    attn_norm = norm_rows(x_float, gain_attn).astype(jnp.bfloat16)
-    seq_rows = lax.all_gather(attn_norm, "tensor", axis=0, tiled=True)
-    qkv_full = lax.all_gather(w_qkv, "dp", axis=1, tiled=True)
+    dp_count, tensor_count = lax.axis_size("dp"), lax.axis_size("tensor")
+    cap_rows = -(-capacity // 16) * 16
+    slots = expert_count * cap_rows
+    heads = w_qkv.shape[2] // DH
+    gather_w = w_qkv.shape[1] % 16 == 0
+    sizes = (dp_count, tensor_count, expert_count, capacity, cap_rows, heads, seq_len // QB, gather_w)
+
     out_rows = lax.all_gather(w_out, "dp", axis=1, tiled=True)
     out_full = lax.all_gather(out_rows, "tensor", axis=0, tiled=True)
     up_full = lax.all_gather(w_up[0], "tensor", axis=0, tiled=True)
@@ -412,50 +570,36 @@
 
     live_mask = lax.dynamic_slice_in_dim(padding.reshape(-1), tensor_pos * rows_local, rows_local)
     live_float = live_mask.astype(jnp.float32)
-    expert_ids = jnp.arange(expert_count, dtype=jnp.int32)
-    pick_first = routes[:, 0:1] == expert_ids[None, :]
-    pick_second = routes[:, 1:2] == expert_ids[None, :]
-    usable = live_mask[:, None] == 1
-    first_hot = (pick_first & usable).astype(jnp.int32)
-    second_hot = (pick_second & usable).astype(jnp.int32)
-    first_place = jnp.sum((jnp.cumsum(first_hot, axis=0) - first_hot) * first_hot, axis=1)
-    second_before = (
-        jnp.cumsum(second_hot, axis=0) - second_hot + jnp.sum(first_hot, axis=0, keepdims=True)
-    )
-    second_place = jnp.sum(second_before * second_hot, axis=1)
-    first_slot = jnp.where(
-        (live_mask == 1) & (first_place < capacity), routes[:, 0] * capacity + first_place, -1
-    )
-    second_slot = jnp.where(
-        (live_mask == 1) & (second_place < capacity), routes[:, 1] * capacity + second_place, -1
-    )
-    slot_ids = jnp.arange(slots, dtype=jnp.int32)
-    select_first = slot_ids[:, None] == first_slot[None, :]
-    select_second = slot_ids[:, None] == second_slot[None, :]
-    select_both = (select_first | select_second).astype(jnp.bfloat16)
-    select_first_low = select_first.astype(jnp.bfloat16)
-    select_second_low = select_second.astype(jnp.bfloat16)
-
-    def to_experts(rows):
-        return lax.all_to_all(rows, "dp", split_axis=0, concat_axis=0, tiled=True)
-
-    grad_rows = jnp.dot(select_both, out_grad, preferred_element_type=jnp.float32)
-    sent_grads = to_experts(grad_rows.astype(jnp.bfloat16).reshape(expert_count, capacity, width))
-    sent_grads = sent_grads.reshape(slots, width)
-
-    heads = qkv_full.shape[2] // DH
-    inner = heads * DH
     table_local = lax.dynamic_slice_in_dim(rel_table, tensor_pos * heads, heads, 1)
     bucket_hot = (rel_bucket[:, None] == jnp.arange(NB, dtype=jnp.int32)[None, :]).astype(jnp.float32)
     line = line_of(jnp.dot(bucket_hot, table_local, precision=HIGHEST).T)
     segk, segq = mask_inputs(segments, padding)
-    qkv_low, heads_low, lse = attend(line, segk, segq, seq_rows, qkv_full)
-    heads_own = lax.all_to_all(heads_low, "tensor", split_axis=0, concat_axis=1, tiled=True)
+    qkv_weight = w_qkv if gather_w else lax.all_gather(w_qkv, "dp", axis=1, tiled=True)
+    seq_rows, qkv_full, qkv_low, lse, heads_all, slot_rows, cot = front(
+        sizes, block_input, gain_attn[None], qkv_weight, out_grad, routes.T, live_mask[None], line, segk, segq
+    )
+    sent_grads = cot.reshape(slots, width)
+    seq_rows = seq_rows.reshape(tensor_count * rows_local, width)
+    qkv_full = qkv_full.reshape(3, width, heads * DH) if gather_w else qkv_weight
+    heads_own = jnp.moveaxis(heads_all, 0, 1).reshape(rows_local, -1)
+
+    expert_ids = jnp.arange(expert_count, dtype=jnp.int32)
+    pick_first = routes[:, 0:1] == expert_ids[None, :]
+    pick_second = routes[:, 1:2] == expert_ids[None, :]
+    slot_ids = jnp.arange(slots, dtype=jnp.int32)
+    select_first = slot_ids[:, None] == slot_rows[0][None, :]
+    select_second = slot_ids[:, None] == slot_rows[1][None, :]
+    select_both = (select_first | select_second).astype(jnp.bfloat16)
+    select_first_low = select_first.astype(jnp.bfloat16)
+    select_second_low = select_second.astype(jnp.bfloat16)
+
+    def to_experts(rows):
+        return lax.all_to_all(rows, "dp", split_axis=0, concat_axis=0, tiled=True)
 
     middle = x_float + jnp.dot(heads_own, out_full, preferred_element_type=jnp.float32)
     moe_low = norm_rows(middle, gain_moe).astype(jnp.bfloat16)
     rows_out = jnp.dot(select_both, moe_low, preferred_element_type=jnp.float32)
-    sent_rows = to_experts(rows_out.astype(jnp.bfloat16).reshape(expert_count, capacity, width))
+    sent_rows = to_experts(rows_out.astype(jnp.bfloat16).reshape(expert_count, cap_rows, width))
     sent_rows = sent_rows.reshape(slots, width)
     logits = jnp.dot(moe_low, w_router, preferred_element_type=jnp.float32)
     first_logit = jnp.sum(jnp.where(pick_first, logits, 0.0), axis=1)
@@ -467,15 +611,15 @@
         + jnp.where(select_second, second_gate[None, :], 0.0),
         axis=1,
     )
-    sent_gates = to_experts(slot_gate.reshape(expert_count, capacity)).reshape(slots, 1)
+    sent_gates = to_experts(slot_gate.reshape(expert_count, cap_rows)).reshape(slots, 1)
 
     act, pre_grad, back, dots = expert_first(sent_rows, sent_grads, up_full, down_full)
-    returned_grad = to_experts(back.reshape(expert_count, capacity, width)).reshape(slots, width)
-    slot_dots = to_experts(dots[0].reshape(expert_count, capacity)).reshape(slots)
+    returned_grad = to_experts(back.reshape(expert_count, cap_rows, width)).reshape(slots, width)
+    slot_dots = to_experts(dots[0].reshape(expert_count, cap_rows)).reshape(slots)
     produced, up_part, down_part = expert_late(
         sent_rows, sent_grads, sent_gates, act, pre_grad, down_full
     )
-    returned = to_experts(produced.reshape(expert_count, capacity, width)).reshape(slots, width)
+    returned = to_experts(produced.reshape(expert_count, cap_rows, width)).reshape(slots, width)
     w_up_grad = lax.psum_scatter(up_part, "tensor", scatter_dimension=0, tiled=True)
     w_down_grad = lax.psum_scatter(down_part, "tensor", scatter_dimension=0, tiled=True)
 

time: 651 us -> 608 us (0.934)
  waiting for transfers between devices: 292 us -> 188 us
  Pallas kernels: 103 us -> 153 us
  blocking collectives: 143 us -> 172 us
  starting transfers between devices: 23.9 us -> 10.7 us
    all_to_all x4 -> x2, waiting for transfers between devices: 169 us -> 80.8 us  [to_experts(): return lax.all_to_all(rows, 'dp', split_axis=0, concat_axis=0, tiled=True)]
    all_to_all x2 -> x3, blocking collectives: 19.9 us -> 82.7 us  [to_experts(): return lax.all_to_all(rows, 'dp', split_axis=0, concat_axis=0, tiled=True)]
    pallas_call x1, Pallas kernels: 18.4 us -> 69 us  [front(): pl.pallas_call(functools.partial(front_kernel, sizes), in_specs=[vmem] *...]
    all_gather x1 -> x0, blocking collectives: 34.1 us -> none  [body(): qkv_full = lax.all_gather(w_qkv, 'dp', axis=1, tiled=True)]
    all_to_all x1 -> x0, waiting for transfers between devices: 17 us -> none  [body(): lax.all_to_all(heads_low, 'tensor', split_axis=0, concat_axis=1, tiled=True)]
    all_to_all x4 -> x2, starting transfers between devices: 19.8 us -> 10.1 us  [to_experts(): return lax.all_to_all(rows, 'dp', split_axis=0, concat_axis=0, tiled=True)]
  transfers between devices with their start and end apart: 15 -> 11, of which waited for: 9 -> 6; matrix products, arithmetic and copies ran while one was open for 7% -> 7% of each run, Pallas kernels for 11% -> 20%
where the time goes in v1:
time: 608 us; the launch traced here: 603 us
  waiting for transfers between devices  188 us (31%)
  blocking collectives  172 us (28%)
  Pallas kernels  153 us (25%)
  matrix products  25.2 us (4%)
  local copies, waits for them, and re-layouts  24.3 us (4%)
  other arithmetic  15.9 us (3%)
  between operations  14.9 us (2%)
  starting transfers between devices  10.7 us (2%)
    all_to_all x3, blocking collectives, to_experts(): return lax.all_to_all(rows, 'dp', split_axis=0, concat_axis=0, tiled=True)  82.7 us
    all_to_all x2, waiting for transfers between devices, to_experts(): return lax.all_to_all(rows, 'dp', split_axis=0, concat_axis=0, tiled=True)  80.8 us
    pallas_call x1, Pallas kernels, front(): pl.pallas_call(functools.partial(front_kernel, sizes), in_specs=[vmem] *...  69 us
    psum x1, blocking collectives, body(): lax.psum((gain_attn_grad, table_whole), ('dp', 'tensor'))  41.9 us
    reduce_scatter x1, waiting for transfers between devices, body(): lax.psum_scatter(norm_part, 'tensor', scatter_dimension=0, tiled=True)  37.7 us
    all_gather x1, blocking collectives, body(): out_rows = lax.all_gather(w_out, 'dp', axis=1, tiled=True)  32.7 us
    pallas_call x1, Pallas kernels, expert_first(): pl.pallas_call(functools.partial(expert_kernel, steps), grid=(steps,), in...  29.8 us
    pallas_call x1, Pallas kernels, attend_back(): pl.pallas_call(functools.partial(attend_back_kernel, heads, blocks, seqs)...  28 us
  transfers between devices with their start and end apart: 11, of which 6 were waited for; matrix products, arithmetic and copies ran while one was open for 7% of the time, Pallas kernels for 20%

profile of v1, /device:TPU:0, one launch (start us, length us, event | category | flops | bytes accessed | tf_op | source)
XLA Modules:
  0.0 603.5 jit_solution(3131963664320920705)
XLA Ops:
  8.1 32.7 %all_gather.12 = bf16[192,768]{0,1:T(8,128)(2,1)S(1)} all-gather(bf16[192,96]{0,1:T(8,128)(2,1)S(1)} %copy.54), channel_id=1, replica_groups=mesh['dp'=8,'tensor'=4] {'dp'}, dimensions={1}, use_global_device_ids=true | all-gather | bytes 331776 | tf_op jit(solution)/shard_map/all_gather | solution.py:566
  48.3 69.0 %front.1 = (bf16[4,512,768]{2,1,0:T(8,128)(2,1)}, bf16[3,8,96,192]{3,2,1,0:T(8,128)(2,1)}, bf16[2,3,1024,192]{3,2,1,0:T(8,128)(2,1)}, f32[2,3,1024]{2,1,0:T(4,12...) custom-call(bf16[512,768]{1,0:T(8,128)(2,1)} %x_ref.1, ...), custom_call_target="tpu_custom_call" | custom-call | flops 20000000000 | bytes 20971520 | tf_op jit(solution)/shard_map/front/pallas_call | solution.py:355
  124.7 62.5 %all_to_all.53 = bf16[8,160,768]{2,1,0:T(8,128)(2,1)S(1)} all-to-all(bf16[8,160,768]{2,1,0:T(8,128)(2,1)S(1)} %bitcast.98), channel_id=1, replica_groups=mesh['dp'=8,'tensor'=4] {'dp'}, dimensions={0} | all-to-all | bytes 3932160 | tf_op jit(solution)/shard_map/all_to_all | solution.py:597
  188.7 29.8 %expert_first.1 = (bf16[1280,3072]{1,0:T(8,128)(2,1)}, bf16[1280,3072]{1,0:T(8,128)(2,1)}, bf16[1280,768]{1,0:T(8,128)(2,1)S(1)}, f32[8,1280]{1,0:T(8,128)S(1)}) custom-call(bf16[1280,768]{1,0:T(8,128)(2,1)S(1)} %bitcast.86, bf16[1280,768]{1,0:T(8,128)(2,1)S(1)} %bitcast.91, bf16[3072,768]{1,0:T(8,128)(2,1)} %bitcast.136, bf16[3072,768]{1,0:T(8,128)(2,1)} %bitcast.134), custom_call_target="tpu_custom_call" | custom-call | flops 18119393280 | bytes 33554432 | tf_op jit(solution)/shard_map/expert_first/pallas_call | solution.py:437
  221.8 10.3 %all_to_all.54 = f32[8,1,160]{2,1,0:T(1,128)} all-to-all(f32[8,1,160]{2,1,0:T(1,128)} %all_to_all.46), channel_id=1, replica_groups=mesh['dp'=8,'tensor'=4] {'dp'}, dimensions={0} | all-to-all | bytes 10240 | tf_op jit(solution)/shard_map/all_to_all | solution.py:597
  232.1 4.3 all-to-all-start.4
  244.5 36.3 %all-to-all-done.4 = bf16[8,160,768]{2,1,0:T(8,128)(2,1)} async-done(((bf16[8,160,768]{2,1,0:T(8,128)(2,1)}), bf16[8,160,768]{2,1,0:T(8,128)(2,1)}, u32[]{:S(2)}, u32[]{:S(2)}) %all-to-all-start.4) | async-done | bytes 1966112 | tf_op jit(solution)/shard_map/all_to_all | solution.py:597
  280.9 3.0 fusion
  284.0 4.1 multiply_reduce_fusion
  291.7 9.9 %all_to_all.55 = f32[8,1,160]{2,1,0:T(1,128)S(1)} all-to-all(f32[8,1,160]{2,1,0:T(1,128)S(1)} %all_to_all.36), channel_id=1, replica_groups=mesh['dp'=8,'tensor'=4] {'dp'}, dimensions={0} | all-to-all | bytes 10240 | tf_op jit(solution)/shard_map/all_to_all | solution.py:597
  302.1 14.2 %reduce-scatter.13.cloned.1.call-done = bf16[192,768]{1,0:T(8,128)(2,1)} async-done(((bf16[768,768]{1,0:T(8,128)(2,1)}), bf16[192,768]{1,0:T(8,128)(2,1)}) %reduce-scatter.13.cloned.1.call-update) | async-done | bytes 294928 | tf_op jit(solution)/shard_map/reduce_scatter | solution.py:653
  318.4 25.8 %expert_late.1 = (bf16[1280,768]{1,0:T(8,128)(2,1)}, bf16[3072,768]{1,0:T(8,128)(2,1)}, bf16[3072,768]{1,0:T(8,128)(2,1)}) custom-call(bf16[1280,768]{1,0:T(8,128)(2,1)S(1)} %bitcast.87, bf16[1280,768]{1,0:T(8,128)(2,1)} %bitcast.90, f32[1280,1]{1,0:T(8,128)S(1)} %reshape.130.gate_ref, bf16[1280,3072]{1,0:T(8,128)(2,1)} %get-tuple-element.30.act_ref, ...), custom_call_target="tpu_custom_call" | custom-call | flops 18119393280 | bytes 33554432 | tf_op jit(solution)/shard_map/expert_late/pallas_call | solution.py:495
  347.2 14.9 %all_to_all.56 = bf16[512,4,192]{0,2,1:T(8,128)(2,1)} all-to-all(bf16[512,4,192]{0,2,1:T(8,128)(2,1)S(1)} %bitcast.97), channel_id=1, replica_groups=mesh['dp'=8,'tensor'=4] {'tensor'}, dimensions={1} | all-to-all | bytes 1572864 | tf_op jit(solution)/shard_map/all_to_all | solution.py:649
  363.6 28.0 %attend_back.1 = (bf16[2048,768]{1,0:T(8,128)(2,1)}, f32[3,768,192]{2,1,0:T(8,128)}, f32[12,8,512]{2,1,0:T(8,128)S(1)}) custom-call(f32[3,1280]{1,0:T(4,128)S(1)} %copy-done.4, s32[2,1024,1]{2,1,0:T(8,128)S(1)} %copy-done.3, s32[2,1,1024]{2,1,0:T(1,128)S(1)} %copy-done.5, bf16[2048,768]{1,0:T(8,128)(2,1)} %bitcast.137, bf16[3,768,192]{2,1,0:T(8,128)(2,1)S(1)} %bitcast.92, ...), custom_call_target="tpu_custom_call" | custom-call | flops 20000000000 | bytes 16777216 | tf_op jit(solution)/shard_map/attend_back/pallas_call | solution.py:128
  391.7 5.8 all-to-all-start.2
  398.0 44.5 %all-to-all-done.2 = bf16[8,160,768]{2,1,0:T(8,128)(2,1)} async-done(((bf16[8,160,768]{2,1,0:T(8,128)(2,1)}), bf16[8,160,768]{2,1,0:T(8,128)(2,1)}, u32[]{:S(2)}, u32[]{:S(2)}) %all-to-all-start.2) | async-done | bytes 1966112 | tf_op jit(solution)/shard_map/all_to_all | solution.py:597
  442.5 3.5 fusion.1
  446.1 4.2 add_add_fusion.1
  454.1 2.9 bitcast_convert_fusion
  457.0 25.2 %reduce-scatter.15.cloned.1.call-done = bf16[768,768]{1,0:T(8,128)(2,1)} async-done(((bf16[3072,768]{1,0:T(8,128)(2,1)}), bf16[768,768]{1,0:T(8,128)(2,1)}) %reduce-scatter.15.cloned.1.call-update) | async-done | bytes 1179664 | tf_op jit(solution)/shard_map/reduce_scatter | solution.py:623
  482.2 2.8 bitcast_convert_fusion.1
  485.0 37.7 %reduce-scatter.9.cloned.1.call-done = bf16[512,768]{1,0:T(8,128)(2,1)} async-done(((bf16[2048,768]{1,0:T(8,128)(2,1)}), bf16[512,768]{1,0:T(8,128)(2,1)}) %reduce-scatter.9.cloned.1.call-update) | async-done | bytes 786448 | tf_op jit(solution)/shard_map/reduce_scatter | solution.py:660
  524.5 41.9 %all-reduce.2 = (f32[32,12]{0,1:T(8,128)}, f32[768]{0:T(1024)}, f32[768]{0:T(1024)}, f32[768,8]{0,1:T(8,128)}) all-reduce(f32[32,12]{0,1:T(8,128)S(1)} %dynamic_update_slice.3, f32[768]{0:T(1024)S(1)} %get-tuple-element.46, f32[768]{0:T(1024)S(1)} %copy-done.46, ...), channel_id=1, replica_groups=mesh['dp'=8,'tensor'=4] {'dp','tensor'}, use_global_device_ids=true, to_apply=%region_13.14 | all-reduce | flops 8064 | bytes 64512 | tf_op jit(solution)/shard_map/psum | solution.py:670
  569.1 27.6 %reduce-scatter.11.cloned.1.call-done = f32[3,96,192]{2,1,0:T(8,128)} async-done(((f32[3,768,192]{2,1,0:T(8,128)}), f32[3,96,192]{2,1,0:T(8,128)}) %reduce-scatter.11.cloned.1.call-update) | async-done | bytes 221200 | tf_op jit(solution)/shard_map/reduce_scatter | solution.py:664
  (209 shorter events, 47.7 us)
Async XLA Ops:
  7.2 230.3 %copy-start = (bf16[768,8]{0,1:T(8,128)(2,1)S(1)}, bf16[768,8]{0,1:T(8,128)(2,1)}, u32[]{:S(2)}) copy-start(bf16[768,8]{0,1:T(8,128)(2,1)} %param.21) | copy-start | bytes 36868
  7.2 112.5 %all-gather.6.cloned.1.call-start = ((), (), s32[]{:S(2)}) async-start(), calls=%async_computation.12 | async-start | bytes 1474560 | tf_op jit(solution)/shard_map/all_gather | solution.py:567
  41.8 145.4 %all-gather.10.cloned.1.call-start = ((), (), s32[]{:S(2)}) async-start(), calls=%async_computation.19 | async-start | bytes 5898240 | tf_op jit(solution)/shard_map/all_gather | solution.py:569
  42.6 144.6 %all-gather.8.cloned.1.call-start = ((), (), s32[]{:S(2)}) async-start(), calls=%async_computation.18 | async-start | bytes 5898240 | tf_op jit(solution)/shard_map/all_gather | solution.py:568
  123.3 114.2 %copy-start.14 = (bf16[512,768]{1,0:T(8,128)(2,1)}, bf16[512,768]{1,0:T(8,128)(2,1)S(1)}, u32[]{:S(2)}) copy-start(bf16[512,768]{1,0:T(8,128)(2,1)S(1)} %multiply_convert_fusion) | copy-start | bytes 2359300
  232.1 48.7 %all-to-all-start.4 = ((bf16[8,160,768]{2,1,0:T(8,128)(2,1)}), bf16[8,160,768]{2,1,0:T(8,128)(2,1)}, u32[]{:S(2)}, u32[]{:S(2)}) async-start(bf16[8,160,768]{2,1,0:T(8,128)(2,1)} %bitcast.88), calls=%async_computation.4 | async-start | bytes 3932160 | tf_op jit(solution)/shard_map/all_to_all | solution.py:597
  236.4 79.8 %reduce-scatter.13.cloned.1.call-start = ((), (), s32[]{:S(2)}) async-start(), calls=%async_computation.15 | async-start | bytes 1474560 | tf_op jit(solution)/shard_map/reduce_scatter | solution.py:653
  238.0 42.8 %copy-start.44 = (s32[1,512]{1,0:T(1,128)S(1)}, s32[1,512]{1,0:T(1,128)}, u32[]{:S(2)}) copy-start(s32[1,512]{1,0:T(1,128)} %copy-done.43) | copy-start | bytes 6148
  238.8 42.0 %copy-start.31 = (f32[512]{0:T(512)}, f32[512]{0:T(512)S(1)}, u32[]{:S(2)}) copy-start(f32[512]{0:T(512)S(1)} %get-tuple-element.67) | copy-start | bytes 6148
  238.8 42.0 %copy-start.33 = (f32[512]{0:T(512)}, f32[512]{0:T(512)S(1)}, u32[]{:S(2)}) copy-start(f32[512]{0:T(512)S(1)} %get-tuple-element.68) | copy-start | bytes 6148
  242.3 38.6 %copy-start.29 = (f32[512]{0:T(512)}, f32[512]{0:T(512)S(1)}, u32[]{:S(2)}) copy-start(f32[512]{0:T(512)S(1)} %subtract_multiply_fusion) | copy-start | bytes 6148
  291.5 161.0 %reduce-scatter.19.cloned.1.call-start = ((), (), s32[]{:S(2)}) async-start(), calls=%async_computation.20 | async-start | bytes 884736
  318.4 135.8 %reduce-scatter.17.cloned.1.call-start = ((), (), s32[]{:S(2)}) async-start(), calls=%async_computation.17 | async-start | bytes 5898240 | tf_op jit(solution)/shard_map/reduce_scatter | solution.py:624
  344.2 138.0 %reduce-scatter.15.cloned.1.call-start = ((), (), s32[]{:S(2)}) async-start(), calls=%async_computation.16 | async-start | bytes 5898240 | tf_op jit(solution)/shard_map/reduce_scatter | solution.py:623
  344.9 177.7 %reduce-scatter.9.cloned.1.call-start = ((), (), s32[]{:S(2)}) async-start(), calls=%async_computation.13 | async-start | bytes 3932160 | tf_op jit(solution)/shard_map/reduce_scatter | solution.py:660
  347.1 16.4 %copy-start.3 = (s32[2,1024,1]{2,1,0:T(8,128)S(1)}, s32[2,1024,1]{2,1,0:T(8,128)}, u32[]{:S(2)}) copy-start(s32[2,1024,1]{2,1,0:T(8,128)} %copy.52.segk_ref) | copy-start | bytes 24580
  347.1 16.4 %copy-start.4 = (f32[3,1280]{1,0:T(4,128)S(1)}, f32[3,1280]{1,0:T(4,128)}, u32[]{:S(2)}) copy-start(f32[3,1280]{1,0:T(4,128)} %concatenate.48.line_ref) | copy-start | bytes 46084
  347.1 16.4 %copy-start.5 = (s32[2,1,1024]{2,1,0:T(1,128)S(1)}, s32[2,1,1024]{2,1,0:T(1,128)}, u32[]{:S(2)}) copy-start(s32[2,1,1024]{2,1,0:T(1,128)} %broadcast_in_dim.112.segq_ref) | copy-start | bytes 24580
  391.7 50.8 %all-to-all-start.2 = ((bf16[8,160,768]{2,1,0:T(8,128)(2,1)}), bf16[8,160,768]{2,1,0:T(8,128)(2,1)}, u32[]{:S(2)}, u32[]{:S(2)}) async-start(bf16[8,160,768]{2,1,0:T(8,128)(2,1)} %bitcast.14), calls=%async_computation.2 | async-start | bytes 3932160 | tf_op jit(solution)/shard_map/all_to_all | solution.py:597
  397.5 45.0 %copy-start.45 = (s32[1,512]{1,0:T(1,128)S(1)}, s32[1,512]{1,0:T(1,128)}, u32[]{:S(2)}) copy-start(s32[1,512]{1,0:T(1,128)} %copy-done.43) | copy-start | bytes 6148
  397.5 199.3 %reduce-scatter.11.cloned.1.call-start = ((), (), s32[]{:S(2)}) async-start(), calls=%async_computation.14 | async-start | bytes 2654208 | tf_op jit(solution)/shard_map/reduce_scatter | solution.py:664
  485.0 39.5 %copy-start.46 = (f32[768]{0:T(1024)S(1)}, f32[768]{0:T(1024)}, u32[]{:S(2)}) copy-start(f32[768]{0:T(1024)} %get-tuple-element.44) | copy-start | bytes 9220
  485.0 81.4 %copy-start.11 = (f32[512,768]{1,0:T(8,128)S(1)}, f32[512,768]{1,0:T(8,128)}, u32[]{:S(2)}) copy-start(f32[512,768]{1,0:T(8,128)} %copy-done.9) | copy-start | bytes 4718596
  566.4 30.4 %copy-start.1 = (bf16[768,8]{0,1:T(8,128)(2,1)S(1)}, bf16[768,8]{0,1:T(8,128)(2,1)}, u32[]{:S(2)}) copy-start(bf16[768,8]{0,1:T(8,128)(2,1)} %param.21) | copy-start | bytes 36868
  (37 other events, 141.4 us)
Sparse Core Ops, SparseCore 0:
  41.9 23.2 all-gather.5
  66.8 50.0 all-gather.9
  118.4 36.5 all-gather.7
  291.6 24.5 reduce-scatter.12
  319.8 62.5 reduce-scatter.18
  384.7 46.8 reduce-scatter.16
  434.3 47.8 reduce-scatter.14
  484.7 37.9 reduce-scatter.8
  527.2 69.5 reduce-scatter.10

commit v2 on v0

--- a/solution.py
+++ b/solution.py
@@ -34,10 +34,10 @@
 
 def score_block(keys, query, tiles, h, qb, segk_ref, segq_ref):
     raw = mm(keys, query, NT)
-    q_seg = segq_ref[0, :, qb * QB : (qb + 1) * QB]
+    q_seg = segq_ref[:, qb * QB : (qb + 1) * QB]
     parts = []
     for kb in range(qb + 1):
-        k_seg = segk_ref[0, kb * QB : (kb + 1) * QB, :]
+        k_seg = segk_ref[kb * QB : (kb + 1) * QB, :]
         same = k_seg == q_seg
         if kb == qb:
             row = lax.broadcasted_iota(jnp.int32, (QB, QB), 0)
@@ -65,7 +65,7 @@
         for h in range(heads):
             cols = slice(h * DH, (h + 1) * DH)
             query = (qkv_ref[0, lower : lower + QB, cols].astype(jnp.float32) * scale).astype(jnp.bfloat16)
-            parts = score_block(qkv_ref[1, 0:nk, cols], query, tiles, h, qb, segk_ref, segq_ref)
+            parts = score_block(qkv_ref[1, 0:nk, cols], query, tiles, h, qb, segk_ref.at[0], segq_ref.at[0])
             peak = functools.reduce(jnp.maximum, [jnp.max(x, axis=0, keepdims=True) for x in parts])
             probs = [jnp.exp(x - peak) for x in parts]
             total = functools.reduce(jnp.add, [jnp.sum(x, axis=0, keepdims=True) for x in probs])
@@ -132,7 +132,7 @@
             query = (qkv_ref[0, lower : lower + QB, cols].astype(jnp.float32) * scale).astype(jnp.bfloat16)
             grad = og_ref[lower : lower + QB, cols]
             lse = lse_ref[0, h : h + 1, lower : lower + QB]
-            parts = score_block(qkv_ref[1, 0:nk, cols], query, tiles, h, qb, segk_ref, segq_ref)
+            parts = score_block(qkv_ref[1, 0:nk, cols], query, tiles, h, qb, segk_ref.at[0], segq_ref.at[0])
             probs = [jnp.exp(x - lse) for x in parts]
             pg = mm(qkv_ref[2, 0:nk, cols], grad, NT)
             pgs = [pg[kb * QB : (kb + 1) * QB] for kb in range(qb + 1)]
@@ -366,6 +366,860 @@
     )(x, g, gate, act, pre, down)
 
 
+MESH = pl.DeviceIdType.MESH
+VMEM_LIMIT = 60 << 20
+
+
+def remote(src, dst, send, recv, axis, place):
+    return pltpu.make_async_remote_copy(
+        src_ref=src, dst_ref=dst, send_sem=send, recv_sem=recv, device_id={axis: place}, device_id_type=MESH
+    )
+
+
+def each_peer(count, step, start=1):
+    if count <= 8:
+        for r in range(start, count):
+            step(r)
+    else:
+        def one(r, carry):
+            step(r)
+            return carry
+        lax.fori_loop(start, count, one, 0)
+
+
+def greet(dp_count, tensor_count):
+    barrier = pltpu.get_barrier_semaphore()
+    dp, tp = lax.axis_index("dp"), lax.axis_index("tensor")
+    for r in range(1, tensor_count):
+        pl.semaphore_signal(barrier, inc=1, device_id={"tensor": lax.rem(tp + r, tensor_count)}, device_id_type=MESH)
+
+    def signal(r):
+        pl.semaphore_signal(barrier, inc=1, device_id={"dp": lax.rem(dp + r, dp_count)}, device_id_type=MESH)
+    each_peer(dp_count, signal)
+    return lambda: pl.semaphore_wait(barrier, tensor_count - 1 + dp_count - 1)
+
+
+def partners(tensor_count):
+    tp = lax.axis_index("tensor")
+    sib = tp + 1 - 2 * lax.rem(tp, 2)
+    return tp, sib, lax.rem(tp + 2, tensor_count), lax.rem(sib + 2, tensor_count)
+
+
+def place_pairs(routes_ref, live_ref, experts, capacity, cap_rows):
+    tokens = live_ref.shape[1]
+    live = live_ref[...] == 1
+    ids = lax.broadcasted_iota(jnp.int32, (experts, tokens), 0)
+    row = lax.broadcasted_iota(jnp.int32, (tokens, tokens), 0)
+    col = lax.broadcasted_iota(jnp.int32, (tokens, tokens), 1)
+    before = (row < col).astype(jnp.float32).astype(jnp.bfloat16)
+    slots = []
+    base = jnp.zeros((experts, 1), jnp.float32)
+    for k in range(2):
+        route = routes_ref[k : k + 1, :]
+        hot = jnp.where((ids == route) & live, 1.0, 0.0)
+        count = mm(hot.astype(jnp.bfloat16), before, NN) + base
+        place = jnp.sum(count * hot, axis=0, keepdims=True).astype(jnp.int32)
+        slots.append(jnp.where(live & (place < capacity), route * cap_rows + place, -1))
+        base = base + jnp.sum(hot, axis=1, keepdims=True)
+    return slots
+
+
+def chosen(first, second, expert, cap_rows):
+    ids = lax.broadcasted_iota(jnp.int32, (cap_rows, first.shape[1]), 0) + expert * cap_rows
+    return jnp.where((ids == first) | (ids == second), 1.0, 0.0).astype(jnp.bfloat16)
+
+
+def attend_sequence(heads, blocks, seq, line_tiles, segk_ref, segq_ref, qkv, heads_out, lse_ref):
+    scale = 1.0 / math.sqrt(DH)
+    for qb in range(blocks):
+        nk = (qb + 1) * QB
+        lower = qb * QB
+        turned = []
+        for h in range(heads):
+            cols = slice(h * DH, (h + 1) * DH)
+            query = (qkv[seq, 0, lower : lower + QB, cols].astype(jnp.float32) * scale).astype(jnp.bfloat16)
+            parts = score_block(qkv[seq, 1, 0:nk, cols], query, line_tiles, h, qb, segk_ref.at[seq], segq_ref.at[seq])
+            peak = functools.reduce(jnp.maximum, [jnp.max(x, axis=0, keepdims=True) for x in parts])
+            probs = [jnp.exp(x - peak) for x in parts]
+            total = functools.reduce(jnp.add, [jnp.sum(x, axis=0, keepdims=True) for x in probs])
+            mixed = functools.reduce(jnp.add, [
+                mm(qkv[seq, 2, kb * QB : (kb + 1) * QB, cols], x.astype(jnp.bfloat16), TN)
+                for kb, x in enumerate(probs)])
+            turned.append(mixed / total)
+            lse_ref[seq, h : h + 1, lower : lower + QB] = peak + jnp.log(total)
+        mixed = jnp.concatenate(turned, axis=0).T.astype(jnp.bfloat16)
+        half = blocks // 2
+        heads_out[seq * 2 + qb // half, (qb % half) * QB : (qb % half + 1) * QB, :] = mixed
+
+
+def front_kernel(sizes, x_ref, gain_ref, w_ref, outw_ref, down_ref, grad_ref, routes_ref, live_ref, line_ref,
+                 segk_ref, segq_ref,
+                 rows, w_all, outw_all, down_all, qkv, lse_ref, heads_all, slots_ref, cot,
+                 tiles, heads_out, cot_send,
+                 far_send, far_recv, w_send, w_recv, o_send, o_recv, ot_send, ot_recv,
+                 dn_send, dn_recv, cot_s, cot_r, head_send, head_recv, local_sem):
+    dp_count, tensor_count, experts, capacity, cap_rows, heads, blocks, gather_w = sizes
+    dp = lax.axis_index("dp")
+    tp, sib, opp, across = partners(tensor_count)
+    wait_barrier = greet(dp_count, tensor_count)
+
+    x = x_ref[...].astype(jnp.float32)
+    r = lax.rsqrt(jnp.mean(x * x, axis=-1, keepdims=True) + EPSILON)
+    rows[tp] = (x * r * gain_ref[...]).astype(jnp.bfloat16)
+    wait_barrier()
+
+    half = rows.shape[1] // 2
+    parts = [pl.ds(0, half), pl.ds(half, half)]
+    far = [remote(rows.at[tp, p], rows.at[tp, p], far_send.at[k], far_recv.at[k], "tensor", opp) for k, p in enumerate(parts)]
+    near = remote(rows.at[tp], rows.at[tp], far_send.at[2], far_recv.at[2], "tensor", sib)
+    onward = [remote(rows.at[opp, p], rows.at[opp, p], far_send.at[3 + k], far_recv.at[3 + k], "tensor", sib) for k, p in enumerate(parts)]
+    for c in far:
+        c.start()
+    near.start()
+
+    def w_copy(r):
+        return remote(w_ref, w_all.at[:, dp], w_send.at[r], w_recv.at[r], "dp", lax.rem(dp + r, dp_count))
+
+    def o_copy(r):
+        return remote(outw_ref, outw_all.at[tp, dp], o_send.at[r], o_recv.at[r], "dp", lax.rem(dp + r, dp_count))
+
+    def ot_copy(k, to):
+        return remote(outw_all.at[tp], outw_all.at[tp], ot_send.at[k], ot_recv.at[k], "tensor", to)
+    if gather_w:
+        each_peer(dp_count, lambda r: w_copy(r).start())
+        each_peer(dp_count, lambda r: o_copy(r).start())
+        own_w = pltpu.make_async_copy(w_ref, w_all.at[:, dp], local_sem.at[0])
+        own_w.start()
+        own_o = pltpu.make_async_copy(outw_ref, outw_all.at[tp, dp], local_sem.at[2])
+        own_o.start()
+
+    first, second = place_pairs(routes_ref, live_ref, experts, capacity, cap_rows)
+    slots_ref[0:1, :] = first
+    slots_ref[1:2, :] = second
+
+    def cot_copy(r):
+        to = lax.rem(dp + r, dp_count)
+        return remote(cot_send.at[to], cot.at[dp], cot_s.at[r], cot_r.at[r], "dp", to)
+
+    def cot_fill(r):
+        to = lax.rem(dp + r, dp_count)
+        cot_send[to] = mm(chosen(first, second, to, cap_rows), grad_ref[...], NN).astype(jnp.bfloat16)
+
+    def cot_go(r):
+        cot_fill(r)
+        cot_copy(r).start()
+    each_peer(dp_count, cot_go)
+    cot_fill(0)
+    own_cot = pltpu.make_async_copy(cot_send.at[dp], cot.at[dp], local_sem.at[1])
+    own_cot.start()
+
+    build_bias(line_ref, tiles, heads, blocks)
+    if gather_w:
+        own_w.wait()
+        each_peer(dp_count, lambda r: w_copy(r).wait_recv())
+    near.wait_recv()
+
+    width = rows.shape[2]
+    own_seq = tp // 2
+    inner = heads * DH
+
+    def project(seq):
+        tokens = rows[pl.ds(seq * 2, 2)].reshape(2 * rows.shape[1], width)
+        for c in range(3):
+            weight = w_all[c].reshape(width, inner) if gather_w else w_ref[c]
+            qkv[seq, c] = mm(tokens, weight, NN).astype(jnp.bfloat16)
+
+    def head_copy(k, to):
+        return remote(heads_out.at[to], heads_all.at[tp], head_send.at[k], head_recv.at[k], "tensor", to)
+
+    own_down = pltpu.make_async_copy(down_ref, down_all.at[tp], local_sem.at[3])
+    down_far = remote(down_ref, down_all.at[tp], dn_send.at[0], dn_recv.at[0], "tensor", opp)
+    down_near = remote(down_ref, down_all.at[tp], dn_send.at[1], dn_recv.at[1], "tensor", sib)
+    down_on = remote(down_all.at[opp], down_all.at[opp], dn_send.at[2], dn_recv.at[2], "tensor", sib)
+
+    project(own_seq)
+    for k in range(2):
+        far[k].wait_recv()
+        onward[k].start()
+    own_down.start()
+    down_far.start()
+    down_near.start()
+    attend_sequence(heads, blocks, own_seq, tiles, segk_ref, segq_ref, qkv, heads_out, lse_ref)
+    head_copy(0, sib).start()
+    heads_all[tp] = heads_out[tp]
+    for k in range(2):
+        onward[k].wait_recv()
+    other = 1 - own_seq
+    project(other)
+    if gather_w:
+        own_o.wait()
+        each_peer(dp_count, lambda r: o_copy(r).wait_recv())
+        for k, to in enumerate((sib, opp, across)):
+            ot_copy(k, to).start()
+    attend_sequence(heads, blocks, other, tiles, segk_ref, segq_ref, qkv, heads_out, lse_ref)
+    head_copy(1, opp).start()
+    head_copy(2, across).start()
+
+    down_far.wait_recv()
+    down_on.start()
+    own_cot.wait()
+    own_down.wait()
+    each_peer(dp_count, lambda r: cot_copy(r).wait())
+    if gather_w:
+        each_peer(dp_count, lambda r: w_copy(r).wait_send())
+        each_peer(dp_count, lambda r: o_copy(r).wait_send())
+        for k, to in enumerate((sib, opp, across)):
+            ot_copy(k, to).wait()
+    for c in far + [near] + onward:
+        c.wait_send()
+    head_copy(0, sib).wait()
+    head_copy(1, opp).wait()
+    head_copy(2, across).wait()
+    down_far.wait_send()
+    down_near.wait()
+    down_on.wait()
+
+
+def sems(*counts):
+    out = []
+    for n in counts:
+        out += [pltpu.SemaphoreType.DMA((n,)), pltpu.SemaphoreType.DMA((n,))]
+    return out
+
+
+def front(sizes, x, gain, w, outw, down, grad, routes_t, live_row, line, segk, segq):
+    dp_count, tensor_count, experts, capacity, cap_rows, heads, blocks, gather_w = sizes
+    tokens, width = x.shape
+    seq_len = blocks * QB
+    seqs = tensor_count * tokens // seq_len
+    inner = heads * DH
+    vmem = pl.BlockSpec(memory_space=pltpu.VMEM)
+    anywhere = pl.BlockSpec(memory_space=pl.ANY)
+    share = width // dp_count
+    return pl.pallas_call(
+        functools.partial(front_kernel, sizes),
+        in_specs=[vmem] * 4 + [anywhere] + [vmem] * 6,
+        out_specs=[vmem] * 3 + [anywhere] + [vmem] * 4 + [anywhere],
+        out_shape=[
+            jax.ShapeDtypeStruct((tensor_count, tokens, width), jnp.bfloat16),
+            jax.ShapeDtypeStruct((3, dp_count, share, inner) if gather_w else (3, 8, 16, 128), jnp.bfloat16),
+            jax.ShapeDtypeStruct((tensor_count, dp_count, share, inner) if gather_w else (3, 8, 16, 128), jnp.bfloat16),
+            jax.ShapeDtypeStruct((tensor_count,) + down.shape, jnp.bfloat16),
+            jax.ShapeDtypeStruct((seqs, 3, seq_len, inner), jnp.bfloat16),
+            jax.ShapeDtypeStruct((seqs, heads, seq_len), jnp.float32),
+            jax.ShapeDtypeStruct((tensor_count, tokens, inner), jnp.bfloat16),
+            jax.ShapeDtypeStruct((8, tokens), jnp.int32),
+            jax.ShapeDtypeStruct((experts, cap_rows, width), jnp.bfloat16),
+        ],
+        scratch_shapes=[
+            pltpu.VMEM((heads, blocks, QB, QB), jnp.float32),
+            pltpu.VMEM((tensor_count, tokens, inner), jnp.bfloat16),
+            pltpu.VMEM((experts, cap_rows, width), jnp.bfloat16),
+        ] + sems(5, dp_count, dp_count, 3, 3, dp_count, 3) + [pltpu.SemaphoreType.DMA((4,))],
+        compiler_params=pltpu.CompilerParams(
+            vmem_limit_bytes=VMEM_LIMIT, collective_id=1, has_side_effects=True),
+        cost_estimate=pl.CostEstimate(flops=20_000_000_000, bytes_accessed=20 << 20, transcendentals=4_000_000),
+        name="front",
+    )(x, gain, w, outw, down, grad, routes_t, live_row, line, segk, segq)
+
+
+def to_row(column, lanes):
+    n = column.shape[0]
+    row = lax.broadcasted_iota(jnp.int32, (n, lanes), 0)
+    col = lax.broadcasted_iota(jnp.int32, (n, lanes), 1)
+    return jnp.sum(jnp.where(row == col, column, 0.0), axis=0, keepdims=True)
+
+
+def to_column(row_values, n):
+    lanes = row_values.shape[1]
+    row = lax.broadcasted_iota(jnp.int32, (n, lanes), 0)
+    col = lax.broadcasted_iota(jnp.int32, (n, lanes), 1)
+    return jnp.sum(jnp.where(row == col, row_values, 0.0), axis=1, keepdims=True)
+
+
+def gate_map(first, second, gate_first, gate_second, expert, cap_rows):
+    ids = lax.broadcasted_iota(jnp.int32, (cap_rows, first.shape[1]), 0) + expert * cap_rows
+    return jnp.where(ids == first, gate_first, jnp.where(ids == second, gate_second, 0.0))
+
+
+def gated_rows(weights, rows):
+    high = weights.astype(jnp.bfloat16)
+    low = (weights - high.astype(jnp.float32)).astype(jnp.bfloat16)
+    return mm(high, rows, TN) + mm(low, rows, TN)
+
+
+def middle_kernel(sizes, x_ref, grad_ref, heads_ref, outw_ref, gain_ref, router_ref, routes_ref, live_ref,
+                  slots_ref, cot_ref, up_ref, down_ref,
+                  up_part, down_part, produced, middle, middle_grad, heads_grad, out_part, stats, gates,
+                  up, down, g_rows, x_rows, x_send, act, side, back_send, back, gate_send, gate_rows,
+                  dot_send, dot_rows, total, moe_low, stage,
+                  up_s, up_r, x_s, x_r, b_s, b_r, g_s, g_r, d_s, d_r, load_sem, stage_sem):
+    dp_count, tensor_count, experts, capacity, cap_rows, heads, blocks, gather_w = sizes
+    dp = lax.axis_index("dp")
+    tp, sib, opp, across = partners(tensor_count)
+    hidden = up.shape[1]
+    tokens, width = x_ref.shape
+    lanes = gate_send.shape[2]
+    wait_barrier = greet(dp_count, tensor_count)
+
+    load_g = pltpu.make_async_copy(cot_ref, g_rows, load_sem.at[0])
+    load_down = pltpu.make_async_copy(down_ref, down, load_sem.at[1])
+    load_up = pltpu.make_async_copy(up_ref, up.at[tp], load_sem.at[2])
+    load_g.start()
+    load_down.start()
+    load_up.start()
+
+    mixed = x_ref[...].astype(jnp.float32)
+    for t in range(tensor_count):
+        mixed = mixed + mm(heads_ref[t], outw_ref[t], NT)
+    middle[...] = mixed
+    r = lax.rsqrt(jnp.mean(mixed * mixed, axis=-1, keepdims=True) + EPSILON)
+    moe_low[...] = (mixed * r * gain_ref[...]).astype(jnp.bfloat16)
+    first, second = slots_ref[0:1, :], slots_ref[1:2, :]
+    wait_barrier()
+
+    def x_copy(r):
+        to = lax.rem(dp + r, dp_count)
+        return remote(x_send.at[to], x_rows.at[dp], x_s.at[r], x_r.at[r], "dp", to)
+
+    def x_go(r):
+        to = lax.rem(dp + r, dp_count)
+        x_send[to] = mm(chosen(first, second, to, cap_rows), moe_low[...], NN).astype(jnp.bfloat16)
+        x_copy(r).start()
+    each_peer(dp_count, x_go)
+    x_rows[dp] = mm(chosen(first, second, dp, cap_rows), moe_low[...], NN).astype(jnp.bfloat16)
+
+    up_far = remote(up_ref, up.at[tp], up_s.at[0], up_r.at[0], "tensor", opp)
+    up_near = remote(up_ref, up.at[tp], up_s.at[1], up_r.at[1], "tensor", sib)
+    up_on = remote(up.at[opp], up.at[opp], up_s.at[2], up_r.at[2], "tensor", sib)
+    up_far.start()
+    up_near.start()
+
+    ids = lax.broadcasted_iota(jnp.int32, (experts, tokens), 0)
+    pick_first, pick_second = ids == routes_ref[0:1, :], ids == routes_ref[1:2, :]
+    live = (live_ref[...] == 1).astype(jnp.float32)
+    logits = mm(router_ref[...], moe_low[...], NT)
+    gap = jnp.sum(jnp.where(pick_first, logits, 0.0) - jnp.where(pick_second, logits, 0.0), axis=0, keepdims=True)
+    gate_first = live / (1.0 + jnp.exp(-gap))
+    gate_second = live / (1.0 + jnp.exp(gap))
+    gates[0:1, :] = gate_first
+    gates[1:2, :] = gate_second
+
+    def gate_copy(r):
+        to = lax.rem(dp + r, dp_count)
+        return remote(gate_send.at[to], gate_rows.at[dp], g_s.at[r], g_r.at[r], "dp", to)
+
+    def gate_fill(r):
+        to = lax.rem(dp + r, dp_count)
+        column = jnp.sum(gate_map(first, second, gate_first, gate_second, to, cap_rows), axis=1, keepdims=True)
+        return jnp.broadcast_to(to_row(column, lanes), (8, lanes))
+
+    def gate_go(r):
+        gate_send[lax.rem(dp + r, dp_count)] = gate_fill(r)
+        gate_copy(r).start()
+    each_peer(dp_count, gate_go)
+    gate_rows[dp] = gate_fill(0)
+
+    load_g.wait()
+    load_down.wait()
+    slots = experts * cap_rows
+    block = slots // 4
+
+    def side_block(k, carry):
+        part = pl.ds(pl.multiple_of(k * block, 16), block)
+        here = g_rows[pl.ds(k * (experts // 4), experts // 4)].reshape(block, width)
+        for t in range(tensor_count):
+            side[part, t * hidden : (t + 1) * hidden] = mm(here, down[t], NT).astype(jnp.bfloat16)
+        return carry
+    lax.fori_loop(0, 4, side_block, 0)
+
+    load_up.wait()
+    up_far.wait_recv()
+    up_on.start()
+    up_near.wait_recv()
+    up_on.wait_recv()
+
+    def back_copy(r):
+        to = lax.rem(dp - r + dp_count, dp_count)
+        return remote(back_send.at[to], back.at[dp], b_s.at[r], b_r.at[r], "dp", to)
+
+    def dot_copy(r):
+        to = lax.rem(dp - r + dp_count, dp_count)
+        return remote(dot_send.at[to], dot_rows.at[dp], d_s.at[r], d_r.at[r], "dp", to)
+
+    group = max(1, min(dp_count, 320 // cap_rows))
+
+    def first_pass(step, carry):
+        rounds = [step * group + k for k in range(group)]
+        froms = [lax.rem(dp - r + dp_count, dp_count) for r in rounds]
+        for k, r in enumerate(rounds):
+            if k == 0:
+                @pl.when(r > 0)
+                def _():
+                    x_copy(r).wait_recv()
+            else:
+                x_copy(r).wait_recv()
+        here = jnp.concatenate([x_rows[s] for s in froms], axis=0)
+        total_back = jnp.zeros((group * cap_rows, width), jnp.float32)
+        dots = jnp.zeros((group * cap_rows, 128), jnp.float32)
+        for t in range(tensor_count):
+            cols = slice(t * hidden, (t + 1) * hidden)
+            pre = mm(here, up[t], NT)
+            value, slope = gelu_pair(pre)
+            low = value.astype(jnp.bfloat16)
+            places = [pl.ds(pl.multiple_of(s * cap_rows, 16), cap_rows) for s in froms]
+            beside = jnp.concatenate([side[p, cols] for p in places], axis=0).astype(jnp.float32)
+            product = low.astype(jnp.float32) * beside
+            dots = dots + sum(product[:, k : k + 128] for k in range(0, hidden, 128))
+            grad = (beside * slope).astype(jnp.bfloat16)
+            for k, p in enumerate(places):
+                piece = slice(k * cap_rows, (k + 1) * cap_rows)
+                act[p, cols] = low[piece]
+                side[p, cols] = grad[piece]
+            total_back = total_back + mm(grad, up[t], NN)
+        column = jnp.sum(dots, axis=1, keepdims=True)
+        for k, (r, s) in enumerate(zip(rounds, froms)):
+            piece = slice(k * cap_rows, (k + 1) * cap_rows)
+            low = total_back[piece].astype(jnp.bfloat16)
+            line = jnp.broadcast_to(to_row(column[piece], lanes), (8, lanes))
+
+            def send():
+                back_send[s] = low
+                dot_send[s] = line
+                back_copy(r).start()
+                dot_copy(r).start()
+
+            def keep():
+                back[dp] = low
+                dot_rows[dp] = line
+            if k == 0:
+                pl.when(r > 0)(send)
+                pl.when(r == 0)(keep)
+            else:
+                send()
+        return carry
+    lax.fori_loop(0, dp_count // group, first_pass, 0)
+
+    each_peer(dp_count, lambda r: gate_copy(r).wait_recv())
+
+    def gate_rows_in(s, carry):
+        column = to_column(gate_rows[s, 0:1, :], cap_rows)
+        x_rows[s] = (x_rows[s].astype(jnp.float32) * column).astype(jnp.bfloat16)
+        g_rows[s] = (g_rows[s].astype(jnp.float32) * column).astype(jnp.bfloat16)
+        return carry
+    lax.fori_loop(0, experts, gate_rows_in, 0)
+
+    def late_pass(t, carry):
+        cols = pl.ds(pl.multiple_of(t * hidden, 128), hidden)
+        for k, (left, right, out) in enumerate(((act, g_rows, down_part), (side, x_rows, up_part))):
+            whole = right[...].reshape(slots, width)
+
+            def put():
+                return pltpu.make_async_copy(stage.at[k], out.at[t], stage_sem.at[k])
+
+            @pl.when(t > 0)
+            def _():
+                put().wait()
+            stage[k] = mm(left[:, cols], whole, TN).astype(jnp.bfloat16)
+            put().start()
+        return carry
+    lax.fori_loop(0, tensor_count, late_pass, 0)
+
+    def produce(k, carry):
+        part = pl.ds(pl.multiple_of(k * block, 16), block)
+        out = jnp.zeros((block, width), jnp.float32)
+        for t in range(tensor_count):
+            out = out + mm(act[part, t * hidden : (t + 1) * hidden], down[t], NN)
+        produced[part, :] = out.astype(jnp.bfloat16)
+        return carry
+    lax.fori_loop(0, 4, produce, 0)
+
+    total[...] = jnp.zeros_like(total)
+
+    def combine(r, carry):
+        dot_first, dot_second = carry
+        e = lax.rem(dp + r, dp_count)
+
+        @pl.when(r > 0)
+        def _():
+            back_copy(r).wait_recv()
+            dot_copy(r).wait_recv()
+        weights = gate_map(first, second, gate_first, gate_second, e, cap_rows)
+        total[...] += gated_rows(weights, back[e])
+        column = to_column(dot_rows[e, 0:1, :], cap_rows)
+        ids = lax.broadcasted_iota(jnp.int32, (cap_rows, tokens), 0) + e * cap_rows
+        dot_first = dot_first + jnp.sum(jnp.where(ids == first, column, 0.0), axis=0, keepdims=True)
+        dot_second = dot_second + jnp.sum(jnp.where(ids == second, column, 0.0), axis=0, keepdims=True)
+        return dot_first, dot_second
+    zero_row = jnp.zeros((1, tokens), jnp.float32)
+    dot_first, dot_second = lax.fori_loop(0, dp_count, combine, (zero_row, zero_row))
+
+    change = gate_first * gate_second * (dot_first - dot_second)
+    logit_grad = (jnp.where(pick_first, change, 0.0) - jnp.where(pick_second, change, 0.0)).astype(jnp.bfloat16)
+    norm_grad = total[...] + mm(logit_grad, router_ref[...], TN)
+    mixed = middle[...]
+    r = lax.rsqrt(jnp.mean(mixed * mixed, axis=-1, keepdims=True) + EPSILON)
+    u = mixed * r
+    du = norm_grad * gain_ref[...]
+    grad = grad_ref[...].astype(jnp.float32) + r * (du - u * jnp.mean(du * u, axis=-1, keepdims=True))
+    middle_grad[...] = grad
+    low = grad.astype(jnp.bfloat16)
+    for t in range(tensor_count):
+        heads_grad[t] = mm(low, outw_ref[t], NN).astype(jnp.bfloat16)
+        out_part[t] = mm(low, heads_ref[t], TN).astype(jnp.bfloat16)
+    stats[0:8, :] = jnp.broadcast_to(jnp.sum(norm_grad * u, axis=0, keepdims=True), (8, width))
+    stats[8:, :] = mm(logit_grad, moe_low[...], NN)
+
+    for k in range(2):
+        out = (down_part, up_part)[k]
+        pltpu.make_async_copy(stage.at[k], out.at[tensor_count - 1], stage_sem.at[k]).wait()
+    up_far.wait_send()
+    up_near.wait_send()
+    up_on.wait_send()
+
+    def drain(r):
+        x_copy(r).wait_send()
+        gate_copy(r).wait_send()
+        back_copy(r).wait_send()
+        dot_copy(r).wait_send()
+    each_peer(dp_count, drain)
+
+
+def middle_pass(sizes, x, grad, heads_all, outw, gain, router_t, routes_t, live_row, slot_rows, cot, up, down_all):
+    dp_count, tensor_count, experts, capacity, cap_rows, heads, blocks, gather_w = sizes
+    tokens, width = x.shape
+    inner = heads * DH
+    hidden = up.shape[0]
+    slots = experts * cap_rows
+    lanes = -(-cap_rows // 128) * 128
+    vmem = pl.BlockSpec(memory_space=pltpu.VMEM)
+    anywhere = pl.BlockSpec(memory_space=pl.ANY)
+    shape = jax.ShapeDtypeStruct
+    low = jnp.bfloat16
+    return pl.pallas_call(
+        functools.partial(middle_kernel, sizes),
+        in_specs=[vmem] * 9 + [anywhere] * 3,
+        out_specs=[anywhere] * 2 + [vmem] * 7,
+        out_shape=[
+            shape((tensor_count, hidden, width), low),
+            shape((tensor_count, hidden, width), low),
+            shape((slots, width), low),
+            shape((tokens, width), jnp.float32),
+            shape((tokens, width), jnp.float32),
+            shape((tensor_count, tokens, inner), low),
+            shape((tensor_count, width, inner), low),
+            shape((8 + experts, width), jnp.float32),
+            shape((8, tokens), jnp.float32),
+        ],
+        scratch_shapes=[
+            pltpu.VMEM((tensor_count, hidden, width), low),
+            pltpu.VMEM((tensor_count, hidden, width), low),
+            pltpu.VMEM((experts, cap_rows, width), low),
+            pltpu.VMEM((experts, cap_rows, width), low),
+            pltpu.VMEM((experts, cap_rows, width), low),
+            pltpu.VMEM((slots, tensor_count * hidden), low),
+            pltpu.VMEM((slots, tensor_count * hidden), low),
+            pltpu.VMEM((experts, cap_rows, width), low),
+            pltpu.VMEM((experts, cap_rows, width), low),
+            pltpu.VMEM((experts, 8, lanes), jnp.float32),
+            pltpu.VMEM((experts, 8, lanes), jnp.float32),
+            pltpu.VMEM((experts, 8, lanes), jnp.float32),
+            pltpu.VMEM((experts, 8, lanes), jnp.float32),
+            pltpu.VMEM((tokens, width), jnp.float32),
+            pltpu.VMEM((tokens, width), low),
+            pltpu.VMEM((2, hidden, width), low),
+        ] + sems(3, dp_count, dp_count, dp_count, dp_count)
+        + [pltpu.SemaphoreType.DMA((3,)), pltpu.SemaphoreType.DMA((2,))],
+        compiler_params=pltpu.CompilerParams(
+            vmem_limit_bytes=VMEM_LIMIT, collective_id=2, has_side_effects=True),
+        cost_estimate=pl.CostEstimate(
+            flops=12 * slots * width * hidden * tensor_count, bytes_accessed=40 << 20, transcendentals=4_000_000),
+        name="middle_pass",
+    )(x, grad, heads_all, outw, gain, router_t, routes_t, live_row, slot_rows, cot, up, down_all)
+
+
+def attend_back_sequence(heads, blocks, seq, tiles, sums, segk_ref, segq_ref, qkv, grads, lse_ref, kg, vg, dq, between):
+    scale = 1.0 / math.sqrt(DH)
+    inner = heads * DH
+    half = blocks // 2
+    for h in range(heads):
+        cols = slice(h * DH, (h + 1) * DH)
+        kg[...] = jnp.zeros_like(kg)
+        vg[...] = jnp.zeros_like(vg)
+        for qb in range(blocks):
+            nk = (qb + 1) * QB
+            lower = qb * QB
+            query = (qkv[seq, 0, lower : lower + QB, cols].astype(jnp.float32) * scale).astype(jnp.bfloat16)
+            grad = grads[seq * 2 + qb // half, (qb % half) * QB : (qb % half + 1) * QB, cols]
+            lse = lse_ref[seq, h : h + 1, lower : lower + QB]
+            parts = score_block(qkv[seq, 1, 0:nk, cols], query, tiles, h, qb, segk_ref.at[seq], segq_ref.at[seq])
+            probs = [jnp.exp(x - lse) for x in parts]
+            pg = mm(qkv[seq, 2, 0:nk, cols], grad, NT)
+            pgs = [pg[kb * QB : (kb + 1) * QB] for kb in range(qb + 1)]
+            delta = functools.reduce(jnp.add, [jnp.sum(p * g, axis=0, keepdims=True) for p, g in zip(probs, pgs)])
+            dqt = jnp.zeros((DH, QB), jnp.float32)
+            for kb in range(qb + 1):
+                rows = slice(kb * QB, (kb + 1) * QB)
+                sg = (probs[kb] * (pgs[kb] - delta)).astype(jnp.bfloat16)
+                sums[h, qb - kb] += sg.astype(jnp.float32)
+                vg[rows] += mm(probs[kb].astype(jnp.bfloat16), grad, NN)
+                kg[rows] += mm(sg, query, NN)
+                dqt = dqt + mm(qkv[seq, 1, rows, cols], sg, TN)
+            dq[lower : lower + QB, h * DH : (h + 1) * DH] = (dqt * scale).T.astype(jnp.bfloat16)
+        dq[:, inner + h * DH : inner + (h + 1) * DH] = kg[...].astype(jnp.bfloat16)
+        dq[:, 2 * inner + h * DH : 2 * inner + (h + 1) * DH] = vg[...].astype(jnp.bfloat16)
+        between(h)
+
+
+def fold_lines(sums, h, blocks):
+    moved = []
+    for d in range(blocks):
+        folded = fold_tile(sums, h, d)
+        line = folded[0:1, :]
+        for s in range(1, 8):
+            line = line + pltpu.roll(folded[s : s + 1, :], 2 * QB - s, 1)
+        moved.append(line)
+    out = []
+    for d in range(blocks):
+        piece = moved[d][:, :QB]
+        if d + 1 < blocks:
+            piece = piece + moved[d + 1][:, QB:]
+        out.append(piece)
+    return jnp.concatenate(out, axis=1)
+
+
+def two_stage_start(send, land, s_sem, r_sem, tensor_count):
+    tp = lax.axis_index("tensor")
+    copies = []
+    for r in range(1, tensor_count):
+        copies.append(remote(send, land.at[r - 1], s_sem.at[r], r_sem.at[r], "tensor", lax.rem(tp + r, tensor_count)))
+    for c in copies:
+        c.start()
+    return copies
+
+
+def last_kernel(sizes, x_ref, gain_ref, middle_ref, mgrad_ref, hgrad_ref, rows, w_ref, qkv, lse_ref, line_ref,
+                segk_ref, segq_ref, produced_ref, slots_ref, gates_ref, early_ref, bucket_ref,
+                out_ref, input_grad_ref, wgrad_ref, early_out, late_out,
+                tiles, sums, kg, vg, dq, grads, landed, npart, near_land, far_land, pair, wsum, wsend, wland,
+                early_land, early_mid, early_dp, late, late_land, late_mid, late_dp, total,
+                h_s, h_r, p_s, p_r, n_s, n_r, w_s, w_r, et_s, et_r, ed_s, ed_r, lt_s, lt_r, ld_s, ld_r):
+    dp_count, tensor_count, experts, capacity, cap_rows, heads, blocks, gather_w = sizes
+    dp = lax.axis_index("dp")
+    tp, sib, opp, across = partners(tensor_count)
+    tokens, width = x_ref.shape
+    inner = heads * DH
+    wait_barrier = greet(dp_count, tensor_count)
+    build_bias(line_ref, tiles, heads, blocks)
+    sums[...] = jnp.zeros_like(sums)
+    own_seq = tp // 2
+    other = 1 - own_seq
+    wait_barrier()
+
+    def h_copy(k, to):
+        return remote(hgrad_ref.at[to], grads.at[tp], h_s.at[k], h_r.at[k], "tensor", to)
+    h_copy(0, opp).start()
+    h_copy(1, across).start()
+    h_copy(2, sib).start()
+    grads[tp] = hgrad_ref[tp]
+
+    def p_copy(r):
+        to = lax.rem(dp - r + dp_count, dp_count)
+        return remote(produced_ref.at[to], landed.at[dp], p_s.at[r], p_r.at[r], "dp", to)
+    each_peer(dp_count, lambda r: p_copy(r).start())
+    landed[dp] = produced_ref[dp]
+
+    early = two_stage_start(early_ref, early_land, et_s, et_r, tensor_count)
+
+    def early_copy(r):
+        return remote(early_mid, early_dp.at[r], ed_s.at[r], ed_r.at[r], "dp", lax.rem(dp + r, dp_count))
+
+    h_copy(0, opp).wait_recv()
+    h_copy(1, across).wait_recv()
+
+    def n_copy(k, src, dst, to):
+        return remote(src, dst, n_s.at[k], n_r.at[k], "tensor", to)
+    pair_near = n_copy(0, npart.at[across], near_land.at[0], sib)
+    pair_far = n_copy(1, pair, far_land, opp)
+    own_near = n_copy(2, npart.at[sib], near_land.at[1], sib)
+
+    def nothing(h):
+        pass
+
+    def project(seq, fresh):
+        here = rows[pl.ds(seq * 2, 2)].reshape(2 * tokens, width)
+        norm = jnp.zeros((2 * tokens, width), jnp.float32)
+        for c in range(3):
+            piece = dq[:, c * inner : (c + 1) * inner]
+            weight = w_ref[c].reshape(width, inner)
+            part = mm(here, piece, TN)
+            wsum[c] = part if fresh else wsum[c] + part
+            norm = norm + mm(piece, weight, NT)
+        column = jnp.sum(norm * here.astype(jnp.float32), axis=0, keepdims=True)
+        low = norm.astype(jnp.bfloat16)
+        npart[seq * 2] = low[:tokens]
+        npart[seq * 2 + 1] = low[tokens:]
+        return column
+
+    attend_back_sequence(heads, blocks, other, tiles, sums, segk_ref, segq_ref, qkv, grads, lse_ref, kg, vg, dq, nothing)
+    gain_row = project(other, True)
+    pair_near.start()
+
+    def between(h):
+        if h == 0:
+            pair_near.wait_recv()
+            pair[...] = (npart[opp].astype(jnp.float32) + near_land[0].astype(jnp.float32)).astype(jnp.bfloat16)
+            pair_far.start()
+            for c in early:
+                c.wait_recv()
+            early_mid[...] = early_ref[...] + early_land[0] + early_land[1] + early_land[2]
+            each_peer(dp_count, lambda r: early_copy(r).start())
+
+    h_copy(2, sib).wait_recv()
+    attend_back_sequence(heads, blocks, own_seq, tiles, sums, segk_ref, segq_ref, qkv, grads, lse_ref, kg, vg, dq, between)
+    gain_row = gain_row + project(own_seq, False)
+    own_near.start()
+
+    def w_copy(r):
+        to = lax.rem(dp + r, dp_count)
+        return remote(wsend.at[to], wland.at[r], w_s.at[r], w_r.at[r], "dp", to)
+    share = width // dp_count
+    for to in range(dp_count):
+        for c in range(3):
+            wsend[to, c] = wsum[c, to * share : (to + 1) * share, :].astype(jnp.bfloat16)
+    each_peer(dp_count, lambda r: w_copy(r).start())
+
+    gain_row = gain_row / gain_ref[...]
+    late[...] = jnp.zeros_like(late)
+    for k in range(width // 128):
+        late[k : k + 1, :] = gain_row[:, k * 128 : (k + 1) * 128]
+    buckets = late.shape[0] - 8
+    ids = lax.broadcasted_iota(jnp.int32, (buckets, bucket_ref.shape[1]), 0)
+    hot = ids == bucket_ref[...]
+    lane = lax.broadcasted_iota(jnp.int32, (buckets, 128), 1)
+    table = jnp.zeros((buckets, 128), jnp.float32)
+    for h in range(heads):
+        column = jnp.sum(jnp.where(hot, fold_lines(sums, h, blocks), 0.0), axis=1, keepdims=True)
+        table = table + jnp.where(lane == tp * heads + h, column, 0.0)
+    late[8:, :] = table
+    late_first = two_stage_start(late, late_land, lt_s, lt_r, tensor_count)
+
+    def late_copy(r):
+        return remote(late_mid, late_dp.at[r], ld_s.at[r], ld_r.at[r], "dp", lax.rem(dp + r, dp_count))
+
+    each_peer(dp_count, lambda r: early_copy(r).wait_recv())
+    summed = early_mid[...]
+    for r in range(1, dp_count):
+        summed = summed + early_dp[r]
+    early_out[...] = summed
+
+    for c in late_first:
+        c.wait_recv()
+    late_mid[...] = late[...] + late_land[0] + late_land[1] + late_land[2]
+    each_peer(dp_count, lambda r: late_copy(r).start())
+
+    first, second = slots_ref[0:1, :], slots_ref[1:2, :]
+    gate_first, gate_second = gates_ref[0:1, :], gates_ref[1:2, :]
+    total[...] = middle_ref[...]
+
+    def combine(r, carry):
+        e = lax.rem(dp + r, dp_count)
+
+        @pl.when(r > 0)
+        def _():
+            p_copy(r).wait_recv()
+        total[...] += gated_rows(gate_map(first, second, gate_first, gate_second, e, cap_rows), landed[e])
+        return carry
+    lax.fori_loop(0, dp_count, combine, 0)
+    out_ref[...] = total[...]
+
+    own_near.wait_recv()
+    pair_far.wait_recv()
+    norm_grad = npart[tp].astype(jnp.float32) + near_land[1].astype(jnp.float32) + far_land[...].astype(jnp.float32)
+    x = x_ref[...].astype(jnp.float32)
+    r = lax.rsqrt(jnp.mean(x * x, axis=-1, keepdims=True) + EPSILON)
+    u = x * r
+    du = norm_grad * gain_ref[...]
+    input_grad_ref[...] = mgrad_ref[...] + r * (du - u * jnp.mean(du * u, axis=-1, keepdims=True))
+
+    each_peer(dp_count, lambda r: w_copy(r).wait_recv())
+    for c in range(3):
+        part = wsum[c, pl.ds(pl.multiple_of(dp * share, 8), share), :]
+        for r in range(1, dp_count):
+            part = part + wland[r, c].astype(jnp.float32)
+        wgrad_ref[c] = part
+
+    each_peer(dp_count, lambda r: late_copy(r).wait_recv())
+    summed = late_mid[...]
+    for r in range(1, dp_count):
+        summed = summed + late_dp[r]
+    late_out[...] = summed
+
+    for c in early + late_first + [pair_near, pair_far, own_near, h_copy(0, opp), h_copy(1, across), h_copy(2, sib)]:
+        c.wait_send()
+
+    def drain(r):
+        p_copy(r).wait_send()
+        early_copy(r).wait_send()
+        w_copy(r).wait_send()
+        late_copy(r).wait_send()
+    each_peer(dp_count, drain)
+
+
+def last_pass(sizes, x, gain, middle, middle_grad, heads_grad, rows, w, qkv, lse, line, segk, segq, produced,
+              slot_rows, gates, early, bucket_row):
+    dp_count, tensor_count, experts, capacity, cap_rows, heads, blocks, gather_w = sizes
+    tokens, width = x.shape
+    inner = heads * DH
+    seq_len = blocks * QB
+    share = width // dp_count
+    vmem = pl.BlockSpec(memory_space=pltpu.VMEM)
+    shape = jax.ShapeDtypeStruct
+    low, full = jnp.bfloat16, jnp.float32
+    late = 8 + NB
+    return pl.pallas_call(
+        functools.partial(last_kernel, sizes),
+        in_specs=[vmem] * 17,
+        out_specs=[vmem] * 5,
+        out_shape=[
+            shape((tokens, width), full),
+            shape((tokens, width), full),
+            shape((3, share, inner), full),
+            shape(early.shape, full),
+            shape((late, 128), full),
+        ],
+        scratch_shapes=[
+            pltpu.VMEM((heads, blocks, QB, QB), full),
+            pltpu.VMEM((heads, blocks, QB, QB), full),
+            pltpu.VMEM((seq_len, DH), full),
+            pltpu.VMEM((seq_len, DH), full),
+            pltpu.VMEM((seq_len, 3 * inner), low),
+            pltpu.VMEM((tensor_count, tokens, inner), low),
+            pltpu.VMEM((experts, cap_rows, width), low),
+            pltpu.VMEM((tensor_count, tokens, width), low),
+            pltpu.VMEM((2, tokens, width), low),
+            pltpu.VMEM((tokens, width), low),
+            pltpu.VMEM((tokens, width), low),
+            pltpu.VMEM((3, width, inner), full),
+            pltpu.VMEM((dp_count, 3, share, inner), low),
+            pltpu.VMEM((dp_count, 3, share, inner), low),
+            pltpu.VMEM((tensor_count - 1,) + early.shape, full),
+            pltpu.VMEM(early.shape, full),
+            pltpu.VMEM((dp_count,) + early.shape, full),
+            pltpu.VMEM((late, 128), full),
+            pltpu.VMEM((tensor_count - 1, late, 128), full),
+            pltpu.VMEM((late, 128), full),
+            pltpu.VMEM((dp_count, late, 128), full),
+            pltpu.VMEM((tokens, width), full),
+        ] + sems(3, dp_count, 3, dp_count, tensor_count, dp_count, tensor_count, dp_count),
+        compiler_params=pltpu.CompilerParams(
+            vmem_limit_bytes=VMEM_LIMIT, collective_id=3, has_side_effects=True),
+        cost_estimate=pl.CostEstimate(flops=30_000_000_000, bytes_accessed=30 << 20, transcendentals=4_000_000),
+        name="last_pass",
+    )(x, gain, middle, middle_grad, heads_grad, rows, w, qkv, lse, line, segk, segq, produced, slot_rows, gates,
+      early, bucket_row)
+
+
 def norm_rows(values, gain):
     return values * lax.rsqrt(jnp.mean(values * values, axis=-1, keepdims=True) + EPSILON) * gain
 
@@ -377,7 +1231,7 @@
     return r * (du - u * jnp.mean(du * u, axis=-1, keepdims=True)), grad * u
 
 
-def body(
+def plain_body(
     block_input,
     out_grad,
     w_qkv,
@@ -539,6 +1393,80 @@
     )
 
 
+def fused_body(
+    block_input,
+    out_grad,
+    w_qkv,
+    w_out,
+    rel_table,
+    gain_attn,
+    gain_moe,
+    w_router,
+    w_up,
+    w_down,
+    routes,
+    segments,
+    padding,
+    rel_bucket,
+):
+    tensor_pos = lax.axis_index("tensor")
+    dp_count, tensor_count = lax.axis_size("dp"), lax.axis_size("tensor")
+    rows_local, width = block_input.shape
+    seq_len = segments.shape[1]
+    heads = w_qkv.shape[2] // DH
+    capacity = slot_capacity(rows_local, w_router.shape[1])
+    expert_count = w_router.shape[1]
+    sizes = (dp_count, tensor_count, expert_count, capacity, capacity, heads, seq_len // QB, True)
+
+    live_row = lax.dynamic_slice_in_dim(padding.reshape(-1), tensor_pos * rows_local, rows_local)[None]
+    routes_t = routes.T
+    table_local = lax.dynamic_slice_in_dim(rel_table, tensor_pos * heads, heads, 1)
+    bucket_hot = (rel_bucket[:, None] == jnp.arange(NB, dtype=jnp.int32)[None, :]).astype(jnp.float32)
+    line = line_of(jnp.dot(bucket_hot, table_local, precision=HIGHEST).T)
+    segk, segq = mask_inputs(segments, padding)
+    rows, w_all, outw, down_all, qkv, lse, heads_all, slot_rows, cot = front(
+        sizes, block_input, gain_attn[None], w_qkv, w_out.T, w_down[0], out_grad, routes_t, live_row, line, segk, segq
+    )
+    outw = outw.reshape(tensor_count, width, -1)
+    up_part, down_part, produced, middle, middle_grad, heads_grad, out_part, early, gates = middle_pass(
+        sizes, block_input, out_grad, heads_all, outw, gain_moe[None], w_router.T, routes_t, live_row,
+        slot_rows, cot, w_up[0], down_all
+    )
+
+    def scattered(part):
+        return lax.psum_scatter(part, "tensor", scatter_dimension=0, tiled=False)
+    w_up_grad = scattered(up_part)
+    w_down_grad = scattered(down_part)
+    w_out_grad = lax.psum_scatter(scattered(out_part).astype(jnp.float32), "dp", scatter_dimension=0, tiled=True)
+    block_output, input_grad, w_qkv_grad, early, late = last_pass(
+        sizes, block_input, gain_attn[None], middle, middle_grad, heads_grad, rows, w_all, qkv, lse, line, segk, segq,
+        produced.reshape(expert_count, capacity, width), slot_rows, gates, early, rel_bucket[None]
+    )
+    return (
+        block_output,
+        input_grad,
+        w_qkv_grad,
+        w_out_grad.T,
+        late[8:, : rel_table.shape[1]],
+        late[: width // 128].reshape(width),
+        early[0],
+        early[8:].T,
+        w_up_grad.astype(jnp.float32)[None],
+        w_down_grad.astype(jnp.float32)[None],
+    )
+
+
+def slot_capacity(tokens, experts):
+    return (10 * tokens + 4 * experts - 1) // (4 * experts)
+
+
+def body(*args):
+    block_input, w_qkv, w_router = args[0], args[2], args[7]
+    capacity = slot_capacity(block_input.shape[0], w_router.shape[1])
+    fits = capacity % 16 == 0 and w_qkv.shape[1] % 16 == 0 and block_input.shape[1] <= 1024
+    return fused_body(*args) if fits else plain_body(*args)
+
+
 def solution(mesh):
     in_specs = (
         P(("dp", "tensor"), None),

time: 651 us -> 519 us (0.80)
  Pallas kernels: 103 us -> 329 us
  waiting for transfers between devices: 292 us -> 137 us
  blocking collectives: 143 us -> 0 us
  matrix products: 25.7 us -> 1.13 us
  starting transfers between devices: 23.9 us -> 0.33 us
  other arithmetic: 19.7 us -> 8.34 us
    pallas_call x4 -> x3, Pallas kernels: 103 us -> 329 us  [the longest x1 136 us: middle_pass(): pl.pallas_call(functools.partial(middle_kernel, sizes), in_specs=[vmem] *...]
    all_to_all x5 -> x0, waiting for transfers between devices: 186 us -> none  [the longest x4 169 us: to_experts(): return lax.all_to_all(rows, 'dp', split_axis=0, concat_axis=0, tiled=True)]
    all_gather x2 -> x0, blocking collectives: 67 us -> none  [the longest x1 34.1 us: body(): qkv_full = lax.all_gather(w_qkv, 'dp', axis=1, tiled=True)]
    psum x1 -> x0, blocking collectives: 41.9 us -> none  [body(): lax.psum((gain_attn_grad, table_whole), ('dp', 'tensor'))]
    all_to_all x3 -> x0, blocking collectives: 33.9 us -> none  [the longest x2 19.9 us: to_experts(): return lax.all_to_all(rows, 'dp', split_axis=0, concat_axis=0, tiled=True)]
    reduce_scatter x5 -> x4, waiting for transfers between devices: 104 us -> 136 us  [the longest x3 134 us: scattered(): return lax.psum_scatter(part, 'tensor', scatter_dimension=0, tiled=False)]
    dot_general x14 -> x1, matrix products: 25.7 us -> 1.13 us  [fused_body(): line = line_of(jnp.dot(bucket_hot, table_local, precision=HIGHEST).T)]
    all_to_all x5 -> x0, starting transfers between devices: 23.3 us -> none  [the longest x4 19.8 us: to_experts(): return lax.all_to_all(rows, 'dp', split_axis=0, concat_axis=0, tiled=True)]
  transfers between devices with their start and end apart: 15 -> 4, of which waited for: 9 -> 4; matrix products, arithmetic and copies ran while one was open for 7% -> 2% of each run, Pallas kernels for 11% -> 19%
where the time goes in v2:
time: 519 us; the launch traced here: 509 us
  Pallas kernels  329 us (63%)
  waiting for transfers between devices  137 us (26%)
  local copies, waits for them, and re-layouts  19.5 us (4%)
  between operations  14.3 us (3%)
  other arithmetic  8.34 us (2%)
    pallas_call x1, Pallas kernels, middle_pass(): pl.pallas_call(functools.partial(middle_kernel, sizes), in_specs=[vmem] *...  136 us
    reduce_scatter x3, waiting for transfers between devices, scattered(): return lax.psum_scatter(part, 'tensor', scatter_dimension=0, tiled=False)  134 us
    pallas_call x1, Pallas kernels, last_pass(): pl.pallas_call(functools.partial(last_kernel, sizes), in_specs=[vmem] * 1...  98.8 us
    pallas_call x1, Pallas kernels, front(): pl.pallas_call(functools.partial(front_kernel, sizes), in_specs=[vmem] *...  94.1 us
  transfers between devices with their start and end apart: 4, of which 4 were waited for; matrix products, arithmetic and copies ran while one was open for 2% of the time, Pallas kernels for 19%

profile of v2, /device:TPU:0, one launch (start us, length us, event | category | flops | bytes accessed | tf_op | source)
XLA Modules:
  0.0 509.2 jit_solution(2848982721708688868)
XLA Ops:
  7.2 1.3 broadcast_in_dim.28.gain_ref
  8.5 1.3 broadcast_in_dim.33.gain_ref
  9.8 1.3 broadcast_in_dim.32.segq_ref
  12.5 1.5 copy.27
  14.0 1.3 copy.28.segk_ref
  16.0 1.1 fusion
  17.8 94.1 %front.1 = (bf16[4,512,768]{2,1,0:T(8,128)(2,1)}, bf16[3,8,96,192]{3,2,1,0:T(8,128)(2,1)}, bf16[4,8,96,192]{3,2,1,0:T(8,128)(2,1)}, bf16[4,768,768]{2,1,0:T(8,12...) custom-call(bf16[512,768]{1,0:T(8,128)(2,1)} %x_ref.5, ...), custom_call_target="tpu_custom_call" | custom-call | flops 20000000000 | bytes 20971520 | tf_op jit(solution)/shard_map/front/pallas_call | solution.py:599
  111.9 136.1 %middle_pass.1 = (bf16[4,768,768]{2,1,0:T(8,128)(2,1)}, bf16[4,768,768]{2,1,0:T(8,128)(2,1)}, bf16[1280,768]{1,0:T(8,128)(2,1)}, f32[512,768]{1,0:T(8,128)}, f32...) custom-call(bf16[512,768]{1,0:T(8,128)(2,1)} %x_ref.5, ...), custom_call_target="tpu_custom_call" | custom-call | flops 36238786560 | bytes 41943040 | tf_op jit(solution)/shard_map/middle_pass/pallas_call | solution.py:899
  248.1 39.0 %reduce-scatter.5.cloned.1.call-done = bf16[1,768,192]{2,1,0:T(8,128)(2,1)} async-done(((bf16[4,768,192]{2,1,0:T(8,128)(2,1)}), bf16[1,768,192]{2,1,0:T(8,128)(2,1)}) %reduce-scatter.5.cloned.1.call-update) | async-done | bytes 294928 | tf_op jit(solution)/shard_map/reduce_scatter | solution.py:1437
  287.0 1.9 bitcast_convert_fusion
  290.3 98.8 %last_pass.1 = (f32[512,768]{1,0:T(8,128)}, f32[512,768]{1,0:T(8,128)}, f32[3,96,192]{2,1,0:T(8,128)}, f32[16,768]{1,0:T(8,128)}, f32[40,128]{1,0:T(8,128)}) custom-call(bf16[512,768]{1,0:T(8,128)(2,1)} %x_ref.5, f32[1,768]{1,0:T(1,128)} %broadcast_in_dim.28.gain_ref, f32[512,768]{1,0:T(8,128)} %get-tuple-element.38.middle_ref, ...), custom_call_target="tpu_custom_call" | custom-call | flops 30000001024 | bytes 31457280 | tf_op jit(solution)/shard_map/last_pass/pallas_call | solution.py:1180
  389.2 0.7 slice.12
  390.6 1.3 slice_reduce_fusion
  391.9 1.3 slice_bitcast_fusion.1
  393.2 1.3 slice_bitcast_fusion
  394.5 1.1 reduce-scatter.7.cloned.1.call-done
  395.7 1.6 copy.30
  397.3 47.9 %reduce-scatter.11.cloned.1.call-done = bf16[1,768,768]{2,1,0:T(8,128)(2,1)} async-done(((bf16[4,768,768]{2,1,0:T(8,128)(2,1)}), bf16[1,768,768]{2,1,0:T(8,128)(2,1)}) %reduce-scatter.11.cloned.1.call-update) | async-done | bytes 1179664 | tf_op jit(solution)/shard_map/reduce_scatter | solution.py:1437
  445.2 2.8 convert_element_type.18
  448.0 47.6 %reduce-scatter.9.cloned.1.call-done = bf16[1,768,768]{2,1,0:T(8,128)(2,1)} async-done(((bf16[4,768,768]{2,1,0:T(8,128)(2,1)}), bf16[1,768,768]{2,1,0:T(8,128)(2,1)}) %reduce-scatter.9.cloned.1.call-update) | async-done | bytes 1179664 | tf_op jit(solution)/shard_map/reduce_scatter | solution.py:1437
  495.6 2.8 convert_element_type.17
  498.4 1.1 copy.38
  499.6 0.8 copy-done.1
  500.4 1.1 copy.39
  (21 shorter events, 5.5 us)
Async XLA Ops:
  7.2 8.8 %copy-start = (f32[32,12]{0,1:T(8,128)S(1)}, f32[32,12]{0,1:T(8,128)}, u32[]{:S(2)}) copy-start(f32[32,12]{0,1:T(8,128)} %param.18) | copy-start | bytes 4612
  7.2 279.9 %reduce-scatter.5.cloned.1.call-start = ((), (), s32[]{:S(2)}) async-start(), calls=%async_computation.4 | async-start | bytes 1966080 | tf_op jit(solution)/shard_map/reduce_scatter | solution.py:1437
  248.0 147.6 %reduce-scatter.7.cloned.1.call-start = ((), (), s32[]{:S(2)}) async-start(), calls=%async_computation.5 | async-start | bytes 884736 | tf_op jit(solution)/shard_map/reduce_scatter | solution.py:1440
  289.0 156.2 %reduce-scatter.11.cloned.1.call-start = ((), (), s32[]{:S(2)}) async-start(), calls=%async_computation.7 | async-start | bytes 5898240 | tf_op jit(solution)/shard_map/reduce_scatter | solution.py:1437
  289.7 205.8 %reduce-scatter.9.cloned.1.call-start = ((), (), s32[]{:S(2)}) async-start(), calls=%async_computation.6 | async-start | bytes 5898240 | tf_op jit(solution)/shard_map/reduce_scatter | solution.py:1437
  448.0 50.4 %copy-start.2 = (f32[512,768]{1,0:T(8,128)S(1)}, f32[512,768]{1,0:T(8,128)}, u32[]{:S(2)}) copy-start(f32[512,768]{1,0:T(8,128)} %get-tuple-element.86) | copy-start | bytes 4718596
  498.4 2.0 copy-start.1
  500.4 1.1 copy-start.3
Sparse Core Ops, SparseCore 0:
  248.2 38.8 reduce-scatter.4
  291.3 104.3 reduce-scatter.6
  398.2 46.9 reduce-scatter.10
  447.7 47.8 reduce-scatter.8
